TPU v7x, 512 devices: a whole 4x4x16 slice. The times are simulated.
512 devices in a mesh: shard: 128 (over z, x, core), help: 4 (over y).
Axes of the slice: x: 4, y: 4, z: 16, core: 2. Of those that a mesh axis runs over, the one named last changes fastest.
Arguments:
- embeds: bfloat16 [65536, 4096], P(('shard', 'help')), may hold values from -6 to 6
- head_rows: bfloat16 [4096, 256], replicated, may hold values from -0.09375 to 0.09375
- cluster_of: int32 [65536], P(('shard', 'help')), may hold values from 0 to 2047, as said below
- owner_of: int32 [2048], replicated, may hold values from 0 to 127, as said below
- live_mask: int32 [65536], P(('shard', 'help')), may hold values 0 or 1
Outputs:
- prefix: bfloat16 [65536, 256], P(('shard', 'help'))
- nearest: float32 [65536], P(('shard', 'help'))
Inputs may be any that keep to these rules, and one draw needn't show every extreme that they name: `cluster_of`: counting rows by the owner (owner_of) of their cluster, the 128 rows of one device include at most 2 rows for any one owner, and exactly 2 for some owner on every device. `owner_of`: every owner holds exactly 16 clusters.
All inputs are finite; a program needn't handle non-finite values. No bound on the sum of `live_mask` on one device may be relied on, other than what follows from the above.
Results may differ from a plain program's by a relative error of at most 0.0011.
Values may be sent and summed in bfloat16 or wider, within the bound.
No kernel may reach another device: no remote copies, remote signals or barrier semaphores. Data moves between devices by JAX's collectives and lax.ppermute only.
A program may use at most 64 MiB of HBM per device.

v0:
```python
import math

import jax
import jax.numpy as jnp
from jax import lax
from jax.sharding import PartitionSpec as P

NORM_EPS = 1e-06


def column_best(best_now, own_rows, own_label, own_index, columns, column_label):
    column_count = columns.shape[0]
    block_rows = math.gcd(column_count, 1024)
    block_count = column_count // block_rows
    column_blocks = columns.reshape(block_count, block_rows, columns.shape[1])
    label_blocks = column_label.reshape(block_count, block_rows)
    offsets = jnp.arange(block_count, dtype=jnp.int32) * block_rows

    def one_block(best_sofar, pieces):
        part_rows, part_label, offset = pieces
        scores = jnp.einsum("ip,jp->ij", own_rows, part_rows, preferred_element_type=jnp.float32)
        column_index = offset + lax.iota(jnp.int32, block_rows)
        allowed = (own_label[:, None] == part_label[None, :]) & (own_label[:, None] >= 0)
        allowed = (
            allowed & (part_label[None, :] >= 0) & (own_index[:, None] != column_index[None, :])
        )
        return (
            jnp.maximum(best_sofar, jnp.max(jnp.where(allowed, scores, jnp.float32(-1.0)), axis=1)),
            None,
        )

    result, _ = lax.scan(one_block, best_now, (column_blocks, label_blocks, offsets))
    return result


def shards(embeds, head_rows, cluster_of, owner_of, live_mask):
    row_count = embeds.shape[0]
    shard_count = lax.axis_size("shard")
    slot_count = 2 * row_count // shard_count
    slab_size = shard_count * slot_count
    projected = jnp.dot(embeds, head_rows, preferred_element_type=jnp.float32)
    prefix = (
        projected * lax.rsqrt(jnp.sum(projected * projected, axis=1, keepdims=True) + NORM_EPS)
    ).astype(jnp.bfloat16)
    cluster_total = owner_of.shape[0]
    cluster_ids = lax.iota(jnp.int32, cluster_total)
    owner_ids = lax.iota(jnp.int32, shard_count)
    matches = cluster_of[:, None] == cluster_ids[None, :]
    owner_row = jnp.sum(jnp.where(matches, owner_of[None, :], 0), axis=1)
    owner_hot = (owner_of[:, None] == owner_ids[None, :]).astype(jnp.int32)
    before_count = jnp.cumsum(owner_hot, axis=0) - owner_hot
    cluster_rank = jnp.sum(before_count * owner_hot, axis=1)
    row_rank = jnp.sum(jnp.where(matches, cluster_rank[None, :], 0), axis=1)
    dest_hot = (owner_row[:, None] == owner_ids[None, :]).astype(jnp.bfloat16)
    row_ids = lax.iota(jnp.int32, row_count)
    earlier = (row_ids[:, None] > row_ids[None, :]).astype(jnp.bfloat16)
    preceding = jnp.dot(earlier, dest_hot, preferred_element_type=jnp.float32)
    slot_pos = jnp.sum(preceding * dest_hot.astype(jnp.float32), axis=1).astype(jnp.int32)
    target = owner_row * slot_count + slot_pos
    row_label = jnp.where(live_mask == 1, row_rank, -1)
    slot_hit = target[:, None] == lax.iota(jnp.int32, slab_size)[None, :]
    slot_tiles = jnp.einsum(
        "rs,rp->sp", slot_hit.astype(jnp.bfloat16), prefix, preferred_element_type=jnp.float32
    ).astype(jnp.bfloat16)
    tile_label = jnp.max(jnp.where(slot_hit, row_label[:, None], -1), axis=0).astype(jnp.bfloat16)
    slot_tiles = slot_tiles.reshape(shard_count, slot_count, slot_tiles.shape[1])
    tile_label = tile_label.reshape(shard_count, slot_count)
    helper = lax.axis_index("help")
    own_index = helper * slab_size + lax.iota(jnp.int32, slab_size)
    starting = jnp.full((slab_size,), -1.0, jnp.float32)
    arrived, arrived_label = (
        lax.all_to_all(slot_tiles, "shard", split_axis=0, concat_axis=0, tiled=True),
        lax.all_to_all(tile_label, "shard", split_axis=0, concat_axis=0, tiled=True),
    )
    own_rows = arrived.reshape(slab_size, arrived.shape[2])
    own_wire_label = arrived_label.reshape(slab_size)
    own_label = own_wire_label.astype(jnp.float32)
    best_cos = column_best(
        starting,
        own_rows,
        own_label,
        own_index,
        lax.all_gather(own_rows, "help", axis=0, tiled=True),
        lax.all_gather(own_wire_label, "help", axis=0, tiled=True).astype(jnp.float32),
    )
    returned = lax.all_to_all(
        best_cos.reshape(shard_count, slot_count), "shard", split_axis=0, concat_axis=0, tiled=True
    )
    row_value = jnp.sum(
        jnp.where(slot_hit, returned.reshape(slab_size)[None, :], jnp.float32(0.0)), axis=1
    )
    nearest = jnp.where(live_mask == 1, row_value, jnp.float32(-1.0))
    return (prefix, nearest)


def solution(mesh):
    return jax.shard_map(
        shards,
        mesh=mesh,
        in_specs=(P(("shard", "help"), None), P(), P(("shard", "help")), P(), P(("shard", "help"))),
        out_specs=(P(("shard", "help"), None), P(("shard", "help"))),
        check_vma=False,
    )
```

profile of v0, /device:TPU:1, one launch (start us, length us, event | category | flops | bytes accessed | tf_op | source)
XLA Modules:
  0.0 103.2 jit_solution(5438614394205146533)
XLA Ops:
  0.6 0.0 copy-start
  0.6 0.9 copy.13
  1.6 0.3 fusion.4
  2.0 0.0 copy-start.3
  2.0 0.1 broadcast_add_fusion
  2.1 0.0 copy-start.4
  2.1 0.0 copy-start.5
  2.1 0.0 copy-start.1
  2.1 0.3 copy.14
  2.5 0.2 copy-done.3
  2.7 0.6 fusion.3
  3.3 0.0 copy-done.4
  3.3 0.4 select_reduce_fusion
  3.7 0.2 fusion.1
  3.9 0.0 copy-done.5
  3.9 0.1 select_reduce_fusion.3
  4.0 0.8 convert_element_type.68
  4.8 20.4 %all-to-all-start = ((bf16[128,1,2]{2,1,0:T(2,128)(2,1)}), bf16[128,1,2]{2,1,0:T(2,128)(2,1)S(1)}, u32[]{:S(2)}, u32[]{:S(2)}) async-start(bf16[128,1,2]{2,1,0:T(2,128)(2,1)} %convert_element_type.68), calls=%async_computation | async-start | bytes 131072 | tf_op jit(solution)/shard_map/all_to_all | solution.py:73
  25.2 0.0 copy-done
  25.2 0.0 copy-done.1
  25.2 0.5 multiply_reduce_fusion
  25.8 0.1 multiply_convert_fusion
  25.9 0.0 copy-start.2
  25.9 0.3 convolution_convert_fusion
  26.2 0.7 reshape.108
  26.9 13.2 %all-to-all-done = bf16[128,1,2]{2,1,0:T(2,128)(2,1)S(1)} async-done(((bf16[128,1,2]{2,1,0:T(2,128)(2,1)}), bf16[128,1,2]{2,1,0:T(2,128)(2,1)S(1)}, u32[]{:S(2)}, u32[]{:S(2)}) %all-to-all-start) | async-done | bytes 544 | tf_op jit(solution)/shard_map/all_to_all | solution.py:73
  40.1 5.7 %all-to-all-start.1 = ((bf16[128,2,256]{2,1,0:T(2,128)(2,1)}), bf16[128,2,256]{2,1,0:T(2,128)(2,1)S(1)}, u32[]{:S(2)}, u32[]{:S(2)}) async-start(bf16[128,2,256]{2,1,0:T(2,128)(2,1)} %reshape.108), calls=%async_computation.1 | async-start | bytes 262144 | tf_op jit(solution)/shard_map/all_to_all | solution.py:72
  45.8 0.2 convert_reduce_fusion
  46.0 0.1 reshape.114
  46.1 0.2 reduce.1
  46.3 0.1 reshape.110
  46.5 8.6 %all-gather = bf16[4,1,256]{2,1,0:T(2,128)(2,1)S(1)} all-gather(bf16[1,1,256]{2,1,0:T(2,128)(2,1)S(1)} %reshape.110), channel_id=1, replica_groups=mesh['shard'=128,'help'=4] {'help'}, dimensions={0}, use_global_device_ids=true | all-gather | bytes 2560 | tf_op jit(solution)/shard_map/all_gather | solution.py:84
  55.1 6.9 %all-to-all-done.1 = bf16[128,2,256]{2,1,0:T(2,128)(2,1)S(1)} async-done(((bf16[128,2,256]{2,1,0:T(2,128)(2,1)}), bf16[128,2,256]{2,1,0:T(2,128)(2,1)S(1)}, u32[]{:S(2)}, u32[]{:S(2)}) %all-to-all-start.1) | async-done | bytes 131104 | tf_op jit(solution)/shard_map/all_to_all | solution.py:72
  61.9 0.1 reshape.109
  62.0 11.5 %all_gather.7 = bf16[1024,256]{1,0:T(8,128)(2,1)S(1)} all-gather(bf16[256,256]{1,0:T(8,128)(2,1)S(1)} %reshape.109), channel_id=1, replica_groups=mesh['shard'=128,'help'=4] {'help'}, dimensions={0}, use_global_device_ids=true | all-gather | bytes 655360 | tf_op jit(solution)/shard_map/all_gather | solution.py:83
  73.4 0.6 fusion
  74.0 0.0 copy-done.2
  74.0 0.1 max.16
  74.2 26.8 %all_to_all.17 = f32[128,1,2]{2,1,0:T(1,128)S(1)} all-to-all(f32[128,1,2]{2,1,0:T(1,128)S(1)} %bitcast.18), channel_id=1, replica_groups=mesh['shard'=128,'help'=4] {'shard'}, dimensions={0} | all-to-all | bytes 2048 | tf_op jit(solution)/shard_map/all_to_all | solution.py:86
  101.0 0.5 broadcast.81
  101.5 0.8 reduce.8
  102.3 0.1 broadcast_in_dim.91
  102.5 0.2 select_reduce_fusion.2
  102.7 0.5 compare_select_fusion
  (11 shorter events, 0.1 us)
Async XLA Ops:
  0.6 24.6 %copy-start = (bf16[4096,256]{1,0:T(8,128)(2,1)S(1)}, bf16[4096,256]{1,0:T(8,128)(2,1)}, u32[]{:S(2)}) copy-start(bf16[4096,256]{1,0:T(8,128)(2,1)} %param.6) | copy-start | bytes 6291460
  2.0 0.7 copy-start.3
  2.1 1.2 %copy-start.4 = (s32[128]{0:T(128)S(1)}, s32[128]{0:T(128)}, u32[]{:S(2)}) copy-start(s32[128]{0:T(128)} %param.7) | copy-start | bytes 1540
  2.1 1.8 %copy-start.5 = (s32[128]{0:T(128)S(1)}, s32[128]{0:T(128)}, u32[]{:S(2)}) copy-start(s32[128]{0:T(128)} %param.9) | copy-start | bytes 1540
  2.1 23.1 %copy-start.1 = (bf16[128,4096]{1,0:T(8,128)(2,1)S(1)}, bf16[128,4096]{1,0:T(8,128)(2,1)}, u32[]{:S(2)}) copy-start(bf16[128,4096]{1,0:T(8,128)(2,1)} %param.5) | copy-start | bytes 3145732
  4.8 35.3 %all-to-all-start = ((bf16[128,1,2]{2,1,0:T(2,128)(2,1)}), bf16[128,1,2]{2,1,0:T(2,128)(2,1)S(1)}, u32[]{:S(2)}, u32[]{:S(2)}) async-start(bf16[128,1,2]{2,1,0:T(2,128)(2,1)} %convert_element_type.68), calls=%async_computation | async-start | bytes 131072 | tf_op jit(solution)/shard_map/all_to_all | solution.py:73
  25.9 48.2 %copy-start.2 = (bf16[128,256]{1,0:T(8,128)(2,1)}, bf16[128,256]{1,0:T(8,128)(2,1)S(1)}, u32[]{:S(2)}) copy-start(bf16[128,256]{1,0:T(8,128)(2,1)S(1)} %multiply_convert_fusion) | copy-start | bytes 196612
  40.1 21.8 %all-to-all-start.1 = ((bf16[128,2,256]{2,1,0:T(2,128)(2,1)}), bf16[128,2,256]{2,1,0:T(2,128)(2,1)S(1)}, u32[]{:S(2)}, u32[]{:S(2)}) async-start(bf16[128,2,256]{2,1,0:T(2,128)(2,1)} %reshape.108), calls=%async_computation.1 | async-start | bytes 262144 | tf_op jit(solution)/shard_map/all_to_all | solution.py:72
where the time goes:
time: 104 us; the launch traced here: 103 us
  blocking collectives  46.8 us (45%)
  starting transfers between devices  26.1 us (25%)
  waiting for transfers between devices  20.1 us (19%)
  local copies, waits for them, and re-layouts  4.16 us (4%)
  other arithmetic  3.56 us (3%)
  matrix products  1.59 us (2%)
    all_to_all x1, blocking collectives, shards(): lax.all_to_all(best_cos.reshape(shard_count, slot_count), 'shard', split_...  26.8 us
    all_to_all x1, starting transfers between devices, shards(): lax.all_to_all(tile_label, 'shard', split_axis=0, concat_axis=0, tiled=True)  20.4 us
    all_to_all x1, waiting for transfers between devices, shards(): lax.all_to_all(tile_label, 'shard', split_axis=0, concat_axis=0, tiled=True)  13.2 us
    all_gather x1, blocking collectives, shards(): lax.all_gather(own_rows, 'help', axis=0, tiled=True)  11.5 us
    all_gather x1, blocking collectives, shards(): lax.all_gather(own_wire_label, 'help', axis=0, tiled=True)  8.55 us
    all_to_all x1, waiting for transfers between devices, shards(): lax.all_to_all(slot_tiles, 'shard', split_axis=0, concat_axis=0, tiled=True)  6.86 us
    all_to_all x1, starting transfers between devices, shards(): lax.all_to_all(slot_tiles, 'shard', split_axis=0, concat_axis=0, tiled=True)  5.71 us
  transfers between devices with their start and end apart: 2, of which 2 were waited for; matrix products, arithmetic and copies ran while one was open for 2% of the time, Pallas kernels for 0%

commit v1 on v0

v1 whole, which is shorter than its diff:
```python
import functools

import jax
import jax.numpy as jnp
from jax import lax
from jax.experimental import pallas as pl
from jax.experimental.pallas import tpu as pltpu
from jax.sharding import Mesh, PartitionSpec as P

NORM_EPS = 1e-06
LANES = 128
PLANES = 16
COLUMNS = 8
HELPERS = 4
SLOTS = 2
PLANE_SLOTS = COLUMNS * SLOTS
SLAB = PLANES * PLANE_SLOTS
OWNER_SLOTS = PLANES * SLOTS
CHUNKS = 4

F32 = jnp.float32
BF16 = jnp.bfloat16


def iota(shape, dim):
    return lax.broadcasted_iota(jnp.int32, shape, dim)


def hot(condition):
    return jnp.where(condition, 1.0, 0.0).astype(BF16)


def dot_nt(left, right):
    return lax.dot_general(left, right, (((1,), (1,)), ((), ())), preferred_element_type=F32)


def dot(left, right):
    return jnp.dot(left, right, preferred_element_type=F32)


def project_kernel(
    embeds, head, cluster_ref, owner_ref, live_ref, prefix_ref, send_ref, target_ref,
    embeds_buf, head_buf, embeds_sem, head_sem,
):
    depth = head_buf.shape[1]
    copies = []
    for part in range(CHUNKS):
        span = pl.ds(part * depth, depth)
        pair = (
            pltpu.make_async_copy(head.at[span, :], head_buf.at[part], head_sem.at[part]),
            pltpu.make_async_copy(embeds.at[:, span], embeds_buf.at[part], embeds_sem.at[part]),
        )
        for copy in pair:
            copy.start()
        copies.append(pair)

    square = (LANES, LANES)
    cluster = cluster_ref[...]
    high, low = cluster >> 7, cluster & 127
    by_low = dot(owner_ref[...].astype(F32).astype(BF16), hot(iota(square, 0) == low))
    owner = jnp.sum(jnp.where(iota(by_low.shape, 0) == high, by_low, 0.0), axis=0, keepdims=True)
    owner = owner.astype(jnp.int32)
    owner_hot = hot(iota(square, 0) == owner)
    same = lax.dot_general(
        owner_hot, owner_hot, (((0,), (0,)), ((), ())), preferred_element_type=F32
    )
    slot = jnp.sum(jnp.where(iota(square, 0) < iota(square, 1), same, 0.0), axis=0, keepdims=True)
    target = owner * SLOTS + slot.astype(jnp.int32)
    target_ref[...] = jnp.broadcast_to(target, target_ref.shape)

    live = live_ref[...] == 1
    high_label = jnp.where(live, high + 1, 0)
    low_label = jnp.where(live, low, 0)
    line = iota(square, 0)
    part = jnp.where((line & 7) == 0, high_label, jnp.where((line & 7) == 1, low_label, 0))
    part = jnp.where((line >> 3) == (target >> 4), part, 0).astype(F32).astype(BF16)
    labels = dot_nt(part, hot(line == (target & 15))).reshape(PLANES, 8, LANES)
    hit = hot(iota((SLAB, LANES), 0) == target)

    projected = jnp.zeros(prefix_ref.shape, F32)
    for part, pair in enumerate(copies):
        for copy in pair:
            copy.wait()
        projected += dot(embeds_buf[part], head_buf[part])
    norm = lax.rsqrt(jnp.sum(projected * projected, axis=1, keepdims=True) + NORM_EPS)
    prefix = (projected * norm).astype(BF16)
    prefix_ref[...] = prefix
    rows = dot(hit, prefix).reshape(PLANES, PLANE_SLOTS, 2 * LANES)
    send_ref[...] = jnp.concatenate(
        [rows[:, :, :LANES], rows[:, :, LANES:], labels], axis=1
    ).astype(BF16)


def sort_kernel(got_ref, send_ref):
    got = got_ref[...].astype(F32)
    low = got[:, :PLANE_SLOTS].reshape(SLAB, LANES).astype(BF16)
    high = got[:, PLANE_SLOTS : 2 * PLANE_SLOTS].reshape(SLAB, LANES).astype(BF16)
    dest = iota((SLAB, SLAB), 0)
    source = ((dest >> 1) & 15) * PLANE_SLOTS + (dest >> 5) * SLOTS + (dest & 1)
    order = hot(iota((SLAB, SLAB), 1) == source)
    rows = dot(order, jnp.concatenate([low, high], axis=1))
    rows = rows.reshape(COLUMNS, OWNER_SLOTS, 2 * LANES)

    square = (LANES, LANES)
    tiles = got[:, 2 * PLANE_SLOTS :].reshape(PLANES * 8, LANES).astype(BF16)
    line, lane = iota(square, 0), iota(square, 1)
    pick = ((line & 31) >> 1) * 8 + (line >> 5)
    spread = dot(hot((lane == pick) & (line < 2 * OWNER_SLOTS)), tiles)
    spread = jnp.where((lane & 1) == (line & 1), spread, 0.0).astype(BF16)
    group = (COLUMNS * 8, LANES)
    labels = dot_nt(hot((iota(group, 1) >> 1) == (iota(group, 0) >> 3)), spread)
    labels = labels.reshape(COLUMNS, 8, LANES)
    out = jnp.concatenate([rows[:, :, :LANES], rows[:, :, LANES:], labels], axis=1).astype(BF16)
    for helper in range(HELPERS):
        send_ref[:, helper] = out


def best_kernel(got_ref, out_ref):
    helper = lax.axis_index("help")
    sources = COLUMNS * HELPERS
    total = sources * OWNER_SLOTS
    low = got_ref[:, :, :OWNER_SLOTS].reshape(total, LANES)
    high = got_ref[:, :, OWNER_SLOTS : 2 * OWNER_SLOTS].reshape(total, LANES)
    columns = jnp.concatenate([low, high], axis=1)
    own_low = got_ref[:, helper, :OWNER_SLOTS].reshape(SLAB, LANES)
    own_high = got_ref[:, helper, OWNER_SLOTS : 2 * OWNER_SLOTS].reshape(SLAB, LANES)

    dest = iota((SLAB, SLAB), 0)
    in_owner = ((dest >> 3) & 15) * SLOTS + (dest >> 7)
    order = hot(iota((SLAB, SLAB), 1) == (dest & 7) * OWNER_SLOTS + in_owner)
    own = dot(order, jnp.concatenate([own_low, own_high], axis=1)).astype(BF16)
    scores = dot_nt(own, columns)

    tiles = got_ref[...].astype(F32)[:, :, 2 * OWNER_SLOTS :].reshape(sources * 8, LANES).astype(BF16)
    shape = (total, sources * 8)
    spread = dot(hot(iota(shape, 1) == (iota(shape, 0) >> 5) * 8), tiles)
    line, lane = iota((total, LANES), 0) & 31, iota((total, LANES), 1)
    spread = jnp.where(lane == line, spread * 128.0, jnp.where(lane == line + 32, spread, 0.0))
    column_label = dot_nt(jnp.ones((8, LANES), BF16), spread.astype(BF16))[:1]

    shape = (SLAB, sources * 8)
    line = iota(shape, 0)
    own_spread = dot(hot(iota(shape, 1) == ((line & 7) * HELPERS + helper) * 8), tiles)
    line, lane = iota((SLAB, LANES), 0), iota((SLAB, LANES), 1)
    line = ((line >> 3) & 15) * SLOTS + (line >> 7)
    own_label = jnp.sum(
        jnp.where(lane == line, own_spread * 128.0, jnp.where(lane == line + 32, own_spread, 0.0)),
        axis=1,
        keepdims=True,
    )
    own_label = jnp.where(own_label > 0.5, own_label, -1.0)
    line = iota((SLAB, 1), 0)
    own_index = ((line & 7) * HELPERS + helper) * OWNER_SLOTS + ((line >> 3) & 15) * SLOTS + (line >> 7)
    allowed = (own_label == column_label) & (own_index != iota((SLAB, total), 1))
    best = jnp.max(jnp.where(allowed, scores, -1.0), axis=1, keepdims=True)
    half = SLAB // 2
    lane = iota(out_ref.shape, 1)
    out_ref[...] = jnp.where(lane == 0, best[:half], jnp.where(lane == 1, best[half:], 0.0))


def finish_kernel(got_ref, target_ref, live_ref, out_ref):
    got = got_ref[...]
    target = target_ref[:1]
    value = jnp.where((target & 1) == 0, got[:, 0:1], got[:, 1:2])
    value = jnp.where(iota(got.shape, 0) == (target >> 1), value, 0.0)
    value = jnp.sum(value, axis=0, keepdims=True)
    out_ref[...] = jnp.where(live_ref[...] == 1, value, -1.0)


VMEM = pl.BlockSpec(memory_space=pltpu.VMEM)
ANY = pl.BlockSpec(memory_space=pl.ANY)
LIMIT = pltpu.CompilerParams(vmem_limit_bytes=32 * 1024 * 1024)


def shards(embeds, head_rows, cluster_of, owner_of, live_mask):
    row_count, width = embeds.shape
    depth = width // CHUNKS
    live = live_mask.reshape(1, row_count)
    prefix, send, target = pl.pallas_call(
        project_kernel,
        out_shape=(
            jax.ShapeDtypeStruct((row_count, 2 * LANES), BF16),
            jax.ShapeDtypeStruct((PLANES, 2 * PLANE_SLOTS + 8, LANES), BF16),
            jax.ShapeDtypeStruct((8, row_count), jnp.int32),
        ),
        in_specs=[ANY, ANY, VMEM, VMEM, VMEM],
        out_specs=(VMEM, VMEM, VMEM),
        scratch_shapes=[
            pltpu.VMEM((CHUNKS, row_count, depth), BF16),
            pltpu.VMEM((CHUNKS, depth, 2 * LANES), BF16),
            pltpu.SemaphoreType.DMA((CHUNKS,)),
            pltpu.SemaphoreType.DMA((CHUNKS,)),
        ],
        compiler_params=LIMIT,
        name="project",
    )(embeds, head_rows, cluster_of.reshape(1, row_count), owner_of.reshape(-1, LANES), live)
    got = lax.all_to_all(send, "z", split_axis=0, concat_axis=0, tiled=True)
    lines = 2 * OWNER_SLOTS + 8
    send = pl.pallas_call(
        sort_kernel,
        out_shape=jax.ShapeDtypeStruct((COLUMNS, HELPERS, lines, LANES), BF16),
        in_specs=[VMEM],
        out_specs=VMEM,
        compiler_params=LIMIT,
        name="sort",
    )(got)
    got = lax.all_to_all(
        send.reshape(COLUMNS * HELPERS, lines, LANES),
        ("x", "core", "help"),
        split_axis=0,
        concat_axis=0,
        tiled=True,
    )
    best = pl.pallas_call(
        best_kernel,
        out_shape=jax.ShapeDtypeStruct((PLANES * COLUMNS, LANES), F32),
        in_specs=[VMEM],
        out_specs=VMEM,
        compiler_params=LIMIT,
        name="best",
    )(got.reshape(COLUMNS, HELPERS, lines, LANES))
    back = lax.all_to_all(best, ("z", "x", "core"), split_axis=0, concat_axis=0, tiled=True)
    nearest = pl.pallas_call(
        finish_kernel,
        out_shape=jax.ShapeDtypeStruct((1, row_count), F32),
        in_specs=[VMEM, VMEM, VMEM],
        out_specs=VMEM,
        compiler_params=LIMIT,
        name="finish",
    )(back, target, live)
    return (prefix, nearest.reshape(row_count))


def solution(mesh):
    axes = ("z", "x", "core", "help")
    fine = Mesh(mesh.devices.reshape(PLANES, 4, 2, HELPERS), axes)
    return jax.shard_map(
        shards,
        mesh=fine,
        in_specs=(P(axes, None), P(), P(axes), P(), P(axes)),
        out_specs=(P(axes, None), P(axes)),
        check_vma=False,
    )
```

time: 104 us -> 83.2 us (0.80)
  blocking collectives: 46.8 us -> 72.9 us
  starting transfers between devices: 26.1 us -> 0 us
  waiting for transfers between devices: 20.1 us -> 0 us
  Pallas kernels: 0 us -> 4.54 us
  other arithmetic: 3.56 us -> 0 us
  matrix products: 1.59 us -> 0 us
    all_to_all x1 -> x3, blocking collectives: 26.8 us -> 72.9 us  [the longest x1 27.8 us: shards(): got = lax.all_to_all(send, 'z', split_axis=0, concat_axis=0, tiled=True)]
    all_to_all x2 -> x0, starting transfers between devices: 26.1 us -> none  [the longest x1 20.4 us: shards(): lax.all_to_all(tile_label, 'shard', split_axis=0, concat_axis=0, tiled=True)]
    all_to_all x2 -> x0, waiting for transfers between devices: 20.1 us -> none  [the longest x1 13.2 us: shards(): lax.all_to_all(tile_label, 'shard', split_axis=0, concat_axis=0, tiled=True)]
    all_gather x2 -> x0, blocking collectives: 20 us -> none  [the longest x1 11.5 us: shards(): lax.all_gather(own_rows, 'help', axis=0, tiled=True)]
    pallas_call x0 -> x4, Pallas kernels: none -> 4.54 us  [the longest x1 2.38 us: shards(): pl.pallas_call(project_kernel, out_shape=(jax.ShapeDtypeStruct((row_count...]
    unnamed x13 -> x10, local copies, waits for them, and re-layouts: 0.41 us -> 4.81 us
    dot_general x4 -> x0, matrix products: 1.59 us -> none  [the longest x1 0.59 us: one_block(): jnp.einsum('ip,jp->ij', own_rows, part_rows, preferred_element_type=jnp.f...]
    reduce_sum x3 -> x0, other arithmetic: 1.16 us -> none  [the longest x1 0.63 us: shards(): cluster_rank = jnp.sum(before_count * owner_hot, axis=1)]
  transfers between devices with their start and end apart: 2 -> 0, of which waited for: 2 -> 0; matrix products, arithmetic and copies ran while one was open for 2% -> 0% of each run, Pallas kernels for 0% -> 0%
where the time goes in v1:
time: 83.2 us; the launch traced here: 82.9 us
  blocking collectives  72.9 us (88%)
  local copies, waits for them, and re-layouts  4.81 us (6%)
  Pallas kernels  4.54 us (5%)
    all_to_all x1, blocking collectives, shards(): got = lax.all_to_all(send, 'z', split_axis=0, concat_axis=0, tiled=True)  27.8 us
    all_to_all x1, blocking collectives, shards(): lax.all_to_all(send.reshape(COLUMNS * HELPERS, lines, LANES), ('x', 'core...  22.8 us
    all_to_all x1, blocking collectives, shards(): lax.all_to_all(best, ('z', 'x', 'core'), split_axis=0, concat_axis=0, til...  22.3 us
    unnamed x10, local copies, waits for them, and re-layouts  4.81 us
    pallas_call x1, Pallas kernels, shards(): pl.pallas_call(project_kernel, out_shape=(jax.ShapeDtypeStruct((row_count...  2.38 us

profile of v1, /device:TPU:1, one launch (start us, length us, event | category | flops | bytes accessed | tf_op | source)
XLA Modules:
  0.0 82.9 jit_solution(2248867936888015206)
XLA Ops:
  0.6 0.0 copy-start
  0.6 1.6 %copy-done = bf16[4096,256]{1,0:T(8,128)(2,1)S(1)} copy-done((bf16[4096,256]{1,0:T(8,128)(2,1)S(1)}, bf16[4096,256]{1,0:T(8,128)(2,1)}, u32[]{:S(2)}) %copy-start) | copy-done | bytes 2097176
  2.2 0.0 copy-start.1
  2.2 1.2 %copy-done.1 = bf16[128,4096]{1,0:T(8,128)(2,1)S(1)} copy-done((bf16[128,4096]{1,0:T(8,128)(2,1)S(1)}, bf16[128,4096]{1,0:T(8,128)(2,1)}, u32[]{:S(2)}) %copy-start.1) | copy-done | bytes 1048600
  3.4 0.0 copy-start.2
  3.5 0.7 copy-done.2
  4.1 0.0 copy-start.3
  4.1 0.7 copy-done.3
  4.8 0.0 copy-start.4
  4.8 0.7 copy-done.4
  5.5 2.4 %project.1 = (bf16[128,256]{1,0:T(8,128)(2,1)}, bf16[16,40,128]{2,1,0:T(8,128)(2,1)S(1)}, s32[8,128]{1,0:T(8,128)S(1)}) custom-call(bf16[128,4096]{1,0:T(8,128)(2,1)S(1)} %copy-done.1, bf16[4096,256]{1,0:T(8,128)(2,1)S(1)} %copy-done, s32[1,128]{1,0:T(1,128)S(1)} %bitcast.17, s32[16,128]{1,0:T(8,128)S(1)} %bitcast.14, s32[1,128]{1,0:T(1,128)S(1)} %bitcast.15), custom_call_target="tpu_custom_call" | custom-call | tf_op jit(solution)/shard_map/project/pallas_call | solution.py:179
  7.8 27.8 %all_to_all.21.got_ref = bf16[16,40,128]{2,1,0:T(8,128)(2,1)S(1)} all-to-all(bf16[16,40,128]{2,1,0:T(8,128)(2,1)S(1)} %get-tuple-element.6), channel_id=1, replica_groups=mesh['z'=16,'x'=4,'core'=2,'help'=4] {'z'}, dimensions={0} | all-to-all | bytes 327680 | tf_op jit(solution)/shard_map/all_to_all | solution.py:197
  35.6 0.3 sort.1
  35.9 22.8 %all_to_all.22 = bf16[32,72,128]{2,1,0:T(8,128)(2,1)S(1)} all-to-all(bf16[32,72,128]{2,1,0:T(8,128)(2,1)S(1)} %bitcast.10), channel_id=1, replica_groups=mesh['z'=16,'x'=4,'core'=2,'help'=4] {'x','core','help'}, dimensions={0} | all-to-all | bytes 1179648 | tf_op jit(solution)/shard_map/all_to_all | solution.py:207
  58.7 1.2 %best.1 = f32[128,128]{1,0:T(8,128)S(1)} custom-call(bf16[8,4,72,128]{3,2,1,0:T(8,128)(2,1)S(1)} %bitcast.11), custom_call_target="tpu_custom_call" | custom-call | tf_op jit(solution)/shard_map/best/pallas_call | solution.py:214
  60.0 22.3 %all_to_all.23 = f32[128,1,128]{2,1,0:T(1,128)S(1)} all-to-all(f32[128,1,128]{2,1,0:T(1,128)S(1)} %bitcast.12), channel_id=1, replica_groups=mesh['z'=16,'x'=4,'core'=2,'help'=4] {'z','x','core'}, dimensions={0} | all-to-all | bytes 131072 | tf_op jit(solution)/shard_map/all_to_all | solution.py:222
  82.3 0.6 finish.1
Async XLA Ops:
  0.6 1.6 %copy-start = (bf16[4096,256]{1,0:T(8,128)(2,1)S(1)}, bf16[4096,256]{1,0:T(8,128)(2,1)}, u32[]{:S(2)}) copy-start(bf16[4096,256]{1,0:T(8,128)(2,1)} %head.1) | copy-start | bytes 6291460
  2.2 1.2 %copy-start.1 = (bf16[128,4096]{1,0:T(8,128)(2,1)S(1)}, bf16[128,4096]{1,0:T(8,128)(2,1)}, u32[]{:S(2)}) copy-start(bf16[128,4096]{1,0:T(8,128)(2,1)} %embeds.1) | copy-start | bytes 3145732
  3.4 0.7 copy-start.2
  4.1 0.7 copy-start.3
  4.8 0.7 copy-start.4

commit v2 on v1

--- a/solution.py
+++ b/solution.py
@@ -39,10 +39,18 @@
 
 
 def project_kernel(
-    embeds, head, cluster_ref, owner_ref, live_ref, prefix_ref, send_ref, target_ref,
-    embeds_buf, head_buf, embeds_sem, head_sem,
+    embeds, head, cluster, owner_of, live_mask, prefix_ref, send_ref, target_ref,
+    embeds_buf, head_buf, cluster_ref, owner_ref, live_ref, embeds_sem, head_sem, index_sem,
 ):
     depth = head_buf.shape[1]
+    index_copies = [
+        pltpu.make_async_copy(source, buf, index_sem.at[spot])
+        for spot, (source, buf) in enumerate(
+            ((cluster, cluster_ref), (owner_of, owner_ref), (live_mask, live_ref))
+        )
+    ]
+    for copy in index_copies:
+        copy.start()
     copies = []
     for part in range(CHUNKS):
         span = pl.ds(part * depth, depth)
@@ -54,6 +62,8 @@
             copy.start()
         copies.append(pair)
 
+    for copy in index_copies:
+        copy.wait()
     square = (LANES, LANES)
     cluster = cluster_ref[...]
     high, low = cluster >> 7, cluster & 127
@@ -183,15 +193,19 @@
             jax.ShapeDtypeStruct((PLANES, 2 * PLANE_SLOTS + 8, LANES), BF16),
             jax.ShapeDtypeStruct((8, row_count), jnp.int32),
         ),
-        in_specs=[ANY, ANY, VMEM, VMEM, VMEM],
+        in_specs=[ANY] * 5,
         out_specs=(VMEM, VMEM, VMEM),
         scratch_shapes=[
             pltpu.VMEM((CHUNKS, row_count, depth), BF16),
             pltpu.VMEM((CHUNKS, depth, 2 * LANES), BF16),
+            pltpu.VMEM((1, row_count), jnp.int32),
+            pltpu.VMEM((owner_of.shape[0] // LANES, LANES), jnp.int32),
+            pltpu.VMEM((1, row_count), jnp.int32),
             pltpu.SemaphoreType.DMA((CHUNKS,)),
             pltpu.SemaphoreType.DMA((CHUNKS,)),
+            pltpu.SemaphoreType.DMA((3,)),
         ],
-        compiler_params=LIMIT,
+        compiler_params=pltpu.CompilerParams(vmem_limit_bytes=60 * 1024 * 1024),
         name="project",
     )(embeds, head_rows, cluster_of.reshape(1, row_count), owner_of.reshape(-1, LANES), live)
     got = lax.all_to_all(send, "z", split_axis=0, concat_axis=0, tiled=True)

time: 83.2 us -> 80 us (0.962)
  local copies, waits for them, and re-layouts: 4.81 us -> 0.01 us
  Pallas kernels: 4.54 us -> 5.96 us
    unnamed x10 -> x4, local copies, waits for them, and re-layouts: 4.81 us -> 0.01 us
    pallas_call x1, Pallas kernels: 2.38 us -> 3.81 us  [shards(): pl.pallas_call(project_kernel, out_shape=(jax.ShapeDtypeStruct((row_count...]
where the time goes in v2:
time: 80 us; the launch traced here: 79.7 us
  blocking collectives  73.1 us (91%)
  Pallas kernels  5.96 us (7%)
    all_to_all x1, blocking collectives, shards(): got = lax.all_to_all(send, 'z', split_axis=0, concat_axis=0, tiled=True)  28 us
    all_to_all x1, blocking collectives, shards(): lax.all_to_all(send.reshape(COLUMNS * HELPERS, lines, LANES), ('x', 'core...  22.8 us
    all_to_all x1, blocking collectives, shards(): lax.all_to_all(best, ('z', 'x', 'core'), split_axis=0, concat_axis=0, til...  22.3 us
    pallas_call x1, Pallas kernels, shards(): pl.pallas_call(project_kernel, out_shape=(jax.ShapeDtypeStruct((row_count...  3.81 us

profile of v2, /device:TPU:1, one launch (start us, length us, event | category | flops | bytes accessed | tf_op | source)
XLA Modules:
  0.0 79.7 jit_solution(15092773030366522077)
XLA Ops:
  0.6 3.8 %project.1 = (bf16[128,256]{1,0:T(8,128)(2,1)}, bf16[16,40,128]{2,1,0:T(8,128)(2,1)}, s32[8,128]{1,0:T(8,128)}) custom-call(bf16[128,4096]{1,0:T(8,128)(2,1)} %embeds.1, bf16[4096,256]{1,0:T(8,128)(2,1)} %head.1, s32[1,128]{1,0:T(1,128)} %bitcast.17, s32[16,128]{1,0:T(8,128)} %bitcast.16, s32[1,128]{1,0:T(1,128)} %bitcast.14), custom_call_target="tpu_custom_call" | custom-call | tf_op jit(solution)/shard_map/project/pallas_call | solution.py:189
  4.4 0.0 copy-start
  4.5 0.0 copy-start.1
  4.5 28.0 %all_to_all.21.got_ref = bf16[16,40,128]{2,1,0:T(8,128)(2,1)S(1)} all-to-all(bf16[16,40,128]{2,1,0:T(8,128)(2,1)} %get-tuple-element.6), channel_id=1, replica_groups=mesh['z'=16,'x'=4,'core'=2,'help'=4] {'z'}, dimensions={0} | all-to-all | bytes 327680 | tf_op jit(solution)/shard_map/all_to_all | solution.py:211
  32.4 0.3 sort.1
  32.7 22.8 %all_to_all.22 = bf16[32,72,128]{2,1,0:T(8,128)(2,1)S(1)} all-to-all(bf16[32,72,128]{2,1,0:T(8,128)(2,1)S(1)} %bitcast.10), channel_id=1, replica_groups=mesh['z'=16,'x'=4,'core'=2,'help'=4] {'x','core','help'}, dimensions={0} | all-to-all | bytes 1179648 | tf_op jit(solution)/shard_map/all_to_all | solution.py:221
  55.6 1.2 %best.1 = f32[128,128]{1,0:T(8,128)S(1)} custom-call(bf16[8,4,72,128]{3,2,1,0:T(8,128)(2,1)S(1)} %bitcast.11), custom_call_target="tpu_custom_call" | custom-call | tf_op jit(solution)/shard_map/best/pallas_call | solution.py:228
  56.8 22.3 %all_to_all.23 = f32[128,1,128]{2,1,0:T(1,128)S(1)} all-to-all(f32[128,1,128]{2,1,0:T(1,128)S(1)} %bitcast.12), channel_id=1, replica_groups=mesh['z'=16,'x'=4,'core'=2,'help'=4] {'z','x','core'}, dimensions={0} | all-to-all | bytes 131072 | tf_op jit(solution)/shard_map/all_to_all | solution.py:236
  79.1 0.0 copy-done
  79.1 0.0 copy-done.1
  79.1 0.6 finish.1
Async XLA Ops:
  4.4 74.7 %copy-start = (s32[8,128]{1,0:T(8,128)S(1)}, s32[8,128]{1,0:T(8,128)}, u32[]{:S(2)}) copy-start(s32[8,128]{1,0:T(8,128)} %get-tuple-element.7.target_ref) | copy-start | bytes 12292
  4.5 74.7 %copy-start.1 = (s32[128]{0:T(128)S(1)}, s32[128]{0:T(128)}, u32[]{:S(2)}) copy-start(s32[128]{0:T(128)} %param.9) | copy-start | bytes 1540

commit v3 on v2

--- a/solution.py
+++ b/solution.py
@@ -17,6 +17,8 @@
 SLAB = PLANES * PLANE_SLOTS
 OWNER_SLOTS = PLANES * SLOTS
 CHUNKS = 4
+PLANE_TURN = 8
+COLUMN_TURN = 4
 
 F32 = jnp.float32
 BF16 = jnp.bfloat16
@@ -76,7 +78,8 @@
     )
     slot = jnp.sum(jnp.where(iota(square, 0) < iota(square, 1), same, 0.0), axis=0, keepdims=True)
     target = owner * SLOTS + slot.astype(jnp.int32)
-    target_ref[...] = jnp.broadcast_to(target, target_ref.shape)
+    target = target ^ (PLANE_TURN * PLANE_SLOTS)
+    target_ref[...] = jnp.broadcast_to(target ^ (COLUMN_TURN * SLOTS), target_ref.shape)
 
     live = live_ref[...] == 1
     high_label = jnp.where(live, high + 1, 0)
@@ -137,7 +140,7 @@
 
     dest = iota((SLAB, SLAB), 0)
     in_owner = ((dest >> 3) & 15) * SLOTS + (dest >> 7)
-    order = hot(iota((SLAB, SLAB), 1) == (dest & 7) * OWNER_SLOTS + in_owner)
+    order = hot(iota((SLAB, SLAB), 1) == ((dest & 7) ^ COLUMN_TURN) * OWNER_SLOTS + in_owner)
     own = dot(order, jnp.concatenate([own_low, own_high], axis=1)).astype(BF16)
     scores = dot_nt(own, columns)
 
@@ -150,7 +153,7 @@
 
     shape = (SLAB, sources * 8)
     line = iota(shape, 0)
-    own_spread = dot(hot(iota(shape, 1) == ((line & 7) * HELPERS + helper) * 8), tiles)
+    own_spread = dot(hot(iota(shape, 1) == (((line & 7) ^ COLUMN_TURN) * HELPERS + helper) * 8), tiles)
     line, lane = iota((SLAB, LANES), 0), iota((SLAB, LANES), 1)
     line = ((line >> 3) & 15) * SLOTS + (line >> 7)
     own_label = jnp.sum(
@@ -160,7 +163,7 @@
     )
     own_label = jnp.where(own_label > 0.5, own_label, -1.0)
     line = iota((SLAB, 1), 0)
-    own_index = ((line & 7) * HELPERS + helper) * OWNER_SLOTS + ((line >> 3) & 15) * SLOTS + (line >> 7)
+    own_index = (((line & 7) ^ COLUMN_TURN) * HELPERS + helper) * OWNER_SLOTS + ((line >> 3) & 15) * SLOTS + (line >> 7)
     allowed = (own_label == column_label) & (own_index != iota((SLAB, total), 1))
     best = jnp.max(jnp.where(allowed, scores, -1.0), axis=1, keepdims=True)
     half = SLAB // 2
@@ -208,7 +211,10 @@
         compiler_params=pltpu.CompilerParams(vmem_limit_bytes=60 * 1024 * 1024),
         name="project",
     )(embeds, head_rows, cluster_of.reshape(1, row_count), owner_of.reshape(-1, LANES), live)
-    got = lax.all_to_all(send, "z", split_axis=0, concat_axis=0, tiled=True)
+    planes = [[spot ^ PLANE_TURN for spot in range(PLANES)]]
+    got = lax.all_to_all(
+        send, "z", split_axis=0, concat_axis=0, tiled=True, axis_index_groups=planes
+    )
     lines = 2 * OWNER_SLOTS + 8
     send = pl.pallas_call(
         sort_kernel,
@@ -233,7 +239,11 @@
         compiler_params=LIMIT,
         name="best",
     )(got.reshape(COLUMNS, HELPERS, lines, LANES))
-    back = lax.all_to_all(best, ("z", "x", "core"), split_axis=0, concat_axis=0, tiled=True)
+    turn = PLANE_TURN * COLUMNS + COLUMN_TURN
+    owners = [[spot ^ turn for spot in range(PLANES * COLUMNS)]]
+    back = lax.all_to_all(
+        best, ("z", "x", "core"), split_axis=0, concat_axis=0, tiled=True, axis_index_groups=owners
+    )
     nearest = pl.pallas_call(
         finish_kernel,
         out_shape=jax.ShapeDtypeStruct((1, row_count), F32),

time: 80 us -> 73.7 us (0.921)
  blocking collectives: 73.1 us -> 66.8 us
    all_to_all x1, blocking collectives: 22.8 us -> 19.3 us  [shards(): lax.all_to_all(send.reshape(COLUMNS * HELPERS, lines, LANES), ('x', 'core...]
    all_to_all x1, blocking collectives: 22.3 us -> 20.1 us  [shards(): lax.all_to_all(best, ('z', 'x', 'core'), split_axis=0, concat_axis=0, til...]
where the time goes in v3:
time: 73.7 us; the launch traced here: 73.5 us
  blocking collectives  66.8 us (91%)
  Pallas kernels  5.96 us (8%)
    all_to_all x1, blocking collectives, shards(): lax.all_to_all(send, 'z', split_axis=0, concat_axis=0, tiled=True, axis_i...  27.4 us
    all_to_all x1, blocking collectives, shards(): lax.all_to_all(best, ('z', 'x', 'core'), split_axis=0, concat_axis=0, til...  20.1 us
    all_to_all x1, blocking collectives, shards(): lax.all_to_all(send.reshape(COLUMNS * HELPERS, lines, LANES), ('x', 'core...  19.3 us
    pallas_call x1, Pallas kernels, shards(): pl.pallas_call(project_kernel, out_shape=(jax.ShapeDtypeStruct((row_count...  3.81 us

profile of v3, /device:TPU:1, one launch (start us, length us, event | category | flops | bytes accessed | tf_op | source)
XLA Modules:
  0.0 73.5 jit_solution(5709564883600848453)
XLA Ops:
  0.6 3.8 %project.1 = (bf16[128,256]{1,0:T(8,128)(2,1)}, bf16[16,40,128]{2,1,0:T(8,128)(2,1)}, s32[8,128]{1,0:T(8,128)}) custom-call(bf16[128,4096]{1,0:T(8,128)(2,1)} %embeds.1, bf16[4096,256]{1,0:T(8,128)(2,1)} %head.1, s32[1,128]{1,0:T(1,128)} %bitcast.17, s32[16,128]{1,0:T(8,128)} %bitcast.16, s32[1,128]{1,0:T(1,128)} %bitcast.14), custom_call_target="tpu_custom_call" | custom-call | tf_op jit(solution)/shard_map/project/pallas_call | solution.py:192
  4.4 0.0 copy-start
  4.5 0.0 copy-start.1
  4.5 27.4 %all_to_all.21.got_ref = bf16[16,40,128]{2,1,0:T(8,128)(2,1)S(1)} all-to-all(bf16[16,40,128]{2,1,0:T(8,128)(2,1)} %get-tuple-element.6), channel_id=1, replica_groups={{256,288,320,352,384,416,448,480,0,32,64,96,128,160,192,224},{257,289,3..., dimensions={0} | all-to-all | bytes 327680 | tf_op jit(solution)/shard_map/all_to_all | solution.py:215
  31.9 0.3 sort.1
  32.2 19.3 %all_to_all.22 = bf16[32,72,128]{2,1,0:T(8,128)(2,1)S(1)} all-to-all(bf16[32,72,128]{2,1,0:T(8,128)(2,1)S(1)} %bitcast.10), channel_id=1, replica_groups=mesh['z'=16,'x'=4,'core'=2,'help'=4] {'x','core','help'}, dimensions={0} | all-to-all | bytes 1179648 | tf_op jit(solution)/shard_map/all_to_all | solution.py:227
  51.5 1.2 %best.1 = f32[128,128]{1,0:T(8,128)S(1)} custom-call(bf16[8,4,72,128]{3,2,1,0:T(8,128)(2,1)S(1)} %bitcast.11), custom_call_target="tpu_custom_call" | custom-call | tf_op jit(solution)/shard_map/best/pallas_call | solution.py:234
  52.7 20.1 %all_to_all.23 = f32[128,1,128]{2,1,0:T(1,128)S(1)} all-to-all(f32[128,1,128]{2,1,0:T(1,128)S(1)} %bitcast.12), channel_id=1, replica_groups={{272,276,280,284,256,260,264,268,304,308,312,316,288,292,296,300,336,34..., dimensions={0} | all-to-all | bytes 131072 | tf_op jit(solution)/shard_map/all_to_all | solution.py:244
  72.8 0.0 copy-done
  72.8 0.0 copy-done.1
  72.8 0.6 finish.1
Async XLA Ops:
  4.4 68.4 %copy-start = (s32[8,128]{1,0:T(8,128)S(1)}, s32[8,128]{1,0:T(8,128)}, u32[]{:S(2)}) copy-start(s32[8,128]{1,0:T(8,128)} %get-tuple-element.7.target_ref) | copy-start | bytes 12292
  4.5 68.4 %copy-start.1 = (s32[128]{0:T(128)S(1)}, s32[128]{0:T(128)}, u32[]{:S(2)}) copy-start(s32[128]{0:T(128)} %param.9) | copy-start | bytes 1540

commit v4 on v3

--- a/solution.py
+++ b/solution.py
@@ -1,5 +1,3 @@
-import functools
-
 import jax
 import jax.numpy as jnp
 from jax import lax
@@ -16,7 +14,7 @@
 PLANE_SLOTS = COLUMNS * SLOTS
 SLAB = PLANES * PLANE_SLOTS
 OWNER_SLOTS = PLANES * SLOTS
-CHUNKS = 4
+PIECES = 2 * PLANE_SLOTS // 8
 PLANE_TURN = 8
 COLUMN_TURN = 4
 
@@ -40,32 +38,7 @@
     return jnp.dot(left, right, preferred_element_type=F32)
 
 
-def project_kernel(
-    embeds, head, cluster, owner_of, live_mask, prefix_ref, send_ref, target_ref,
-    embeds_buf, head_buf, cluster_ref, owner_ref, live_ref, embeds_sem, head_sem, index_sem,
-):
-    depth = head_buf.shape[1]
-    index_copies = [
-        pltpu.make_async_copy(source, buf, index_sem.at[spot])
-        for spot, (source, buf) in enumerate(
-            ((cluster, cluster_ref), (owner_of, owner_ref), (live_mask, live_ref))
-        )
-    ]
-    for copy in index_copies:
-        copy.start()
-    copies = []
-    for part in range(CHUNKS):
-        span = pl.ds(part * depth, depth)
-        pair = (
-            pltpu.make_async_copy(head.at[span, :], head_buf.at[part], head_sem.at[part]),
-            pltpu.make_async_copy(embeds.at[:, span], embeds_buf.at[part], embeds_sem.at[part]),
-        )
-        for copy in pair:
-            copy.start()
-        copies.append(pair)
-
-    for copy in index_copies:
-        copy.wait()
+def scatter_kernel(prefix_ref, cluster_ref, owner_ref, live_ref, send_ref, target_ref):
     square = (LANES, LANES)
     cluster = cluster_ref[...]
     high, low = cluster >> 7, cluster & 127
@@ -88,26 +61,22 @@
     part = jnp.where((line & 7) == 0, high_label, jnp.where((line & 7) == 1, low_label, 0))
     part = jnp.where((line >> 3) == (target >> 4), part, 0).astype(F32).astype(BF16)
     labels = dot_nt(part, hot(line == (target & 15))).reshape(PLANES, 8, LANES)
-    hit = hot(iota((SLAB, LANES), 0) == target)
-
-    projected = jnp.zeros(prefix_ref.shape, F32)
-    for part, pair in enumerate(copies):
-        for copy in pair:
-            copy.wait()
-        projected += dot(embeds_buf[part], head_buf[part])
-    norm = lax.rsqrt(jnp.sum(projected * projected, axis=1, keepdims=True) + NORM_EPS)
-    prefix = (projected * norm).astype(BF16)
-    prefix_ref[...] = prefix
-    rows = dot(hit, prefix).reshape(PLANES, PLANE_SLOTS, 2 * LANES)
+
+    rows = dot(hot(iota((SLAB, LANES), 0) == target), prefix_ref[...])
+    rows = rows.reshape(PLANES, PLANE_SLOTS, 2 * LANES)
+    rows = jnp.concatenate([rows[:, :, :LANES], rows[:, :, LANES:]], axis=1)
+    rows = rows.reshape(PLANES, PIECES, 8, LANES)
     send_ref[...] = jnp.concatenate(
-        [rows[:, :, :LANES], rows[:, :, LANES:], labels], axis=1
+        [rows[:, :, :4], rows[:, :, 4:], labels[:, :4].reshape(PLANES, 1, 4, LANES)], axis=1
     ).astype(BF16)
 
 
 def sort_kernel(got_ref, send_ref):
-    got = got_ref[...].astype(F32)
+    pieces = got_ref[...].astype(F32)
+    got = jnp.concatenate([pieces[:, :PIECES], pieces[:, PIECES : 2 * PIECES]], axis=2)
+    got = got.reshape(PLANES, 2 * PLANE_SLOTS, LANES)
     low = got[:, :PLANE_SLOTS].reshape(SLAB, LANES).astype(BF16)
-    high = got[:, PLANE_SLOTS : 2 * PLANE_SLOTS].reshape(SLAB, LANES).astype(BF16)
+    high = got[:, PLANE_SLOTS:].reshape(SLAB, LANES).astype(BF16)
     dest = iota((SLAB, SLAB), 0)
     source = ((dest >> 1) & 15) * PLANE_SLOTS + (dest >> 5) * SLOTS + (dest & 1)
     order = hot(iota((SLAB, SLAB), 1) == source)
@@ -115,7 +84,8 @@
     rows = rows.reshape(COLUMNS, OWNER_SLOTS, 2 * LANES)
 
     square = (LANES, LANES)
-    tiles = got[:, 2 * PLANE_SLOTS :].reshape(PLANES * 8, LANES).astype(BF16)
+    tiles = pieces[:, 2 * PIECES].reshape(PLANES, 4, LANES)
+    tiles = jnp.concatenate([tiles, tiles], axis=1).reshape(PLANES * 8, LANES).astype(BF16)
     line, lane = iota(square, 0), iota(square, 1)
     pick = ((line & 31) >> 1) * 8 + (line >> 5)
     spread = dot(hot((lane == pick) & (line < 2 * OWNER_SLOTS)), tiles)
@@ -181,36 +151,26 @@
 
 
 VMEM = pl.BlockSpec(memory_space=pltpu.VMEM)
-ANY = pl.BlockSpec(memory_space=pl.ANY)
 LIMIT = pltpu.CompilerParams(vmem_limit_bytes=32 * 1024 * 1024)
 
 
 def shards(embeds, head_rows, cluster_of, owner_of, live_mask):
-    row_count, width = embeds.shape
-    depth = width // CHUNKS
+    row_count = embeds.shape[0]
     live = live_mask.reshape(1, row_count)
-    prefix, send, target = pl.pallas_call(
-        project_kernel,
+    projected = jnp.dot(embeds, head_rows, preferred_element_type=F32)
+    norm = lax.rsqrt(jnp.sum(projected * projected, axis=1, keepdims=True) + NORM_EPS)
+    prefix = (projected * norm).astype(BF16)
+    send, target = pl.pallas_call(
+        scatter_kernel,
         out_shape=(
-            jax.ShapeDtypeStruct((row_count, 2 * LANES), BF16),
-            jax.ShapeDtypeStruct((PLANES, 2 * PLANE_SLOTS + 8, LANES), BF16),
+            jax.ShapeDtypeStruct((PLANES, 2 * PIECES + 1, 4, LANES), BF16),
             jax.ShapeDtypeStruct((8, row_count), jnp.int32),
         ),
-        in_specs=[ANY] * 5,
-        out_specs=(VMEM, VMEM, VMEM),
-        scratch_shapes=[
-            pltpu.VMEM((CHUNKS, row_count, depth), BF16),
-            pltpu.VMEM((CHUNKS, depth, 2 * LANES), BF16),
-            pltpu.VMEM((1, row_count), jnp.int32),
-            pltpu.VMEM((owner_of.shape[0] // LANES, LANES), jnp.int32),
-            pltpu.VMEM((1, row_count), jnp.int32),
-            pltpu.SemaphoreType.DMA((CHUNKS,)),
-            pltpu.SemaphoreType.DMA((CHUNKS,)),
-            pltpu.SemaphoreType.DMA((3,)),
-        ],
-        compiler_params=pltpu.CompilerParams(vmem_limit_bytes=60 * 1024 * 1024),
-        name="project",
-    )(embeds, head_rows, cluster_of.reshape(1, row_count), owner_of.reshape(-1, LANES), live)
+        in_specs=[VMEM] * 4,
+        out_specs=(VMEM, VMEM),
+        compiler_params=LIMIT,
+        name="scatter",
+    )(prefix, cluster_of.reshape(1, row_count), owner_of.reshape(-1, LANES), live)
     planes = [[spot ^ PLANE_TURN for spot in range(PLANES)]]
     got = lax.all_to_all(
         send, "z", split_axis=0, concat_axis=0, tiled=True, axis_index_groups=planes

time: 73.7 us -> 73 us (level)
  Pallas kernels: 5.96 us -> 2.69 us
  matrix products: 0 us -> 1.76 us
  local copies, waits for them, and re-layouts: 0.01 us -> 1.59 us
  blocking collectives: 66.8 us -> 65.9 us
    pallas_call x1, Pallas kernels: 3.81 us -> 0.53 us  [shards(): pl.pallas_call(scatter_kernel, out_shape=(jax.ShapeDtypeStruct((PLANES, 2...]
    dot_general x0 -> x1, matrix products: none -> 1.76 us  [shards(): projected = jnp.dot(embeds, head_rows, preferred_element_type=F32)]
    unnamed x4 -> x10, local copies, waits for them, and re-layouts: 0.01 us -> 1.59 us
    all_to_all x1, blocking collectives: 27.4 us -> 26.1 us  [shards(): lax.all_to_all(send, 'z', split_axis=0, concat_axis=0, tiled=True, axis_i...]
where the time goes in v4:
time: 73 us; the launch traced here: 72.8 us
  blocking collectives  65.9 us (90%)
  Pallas kernels  2.69 us (4%)
  matrix products  1.76 us (2%)
  local copies, waits for them, and re-layouts  1.59 us (2%)
    all_to_all x1, blocking collectives, shards(): lax.all_to_all(send, 'z', split_axis=0, concat_axis=0, tiled=True, axis_i...  26.1 us
    all_to_all x1, blocking collectives, shards(): lax.all_to_all(best, ('z', 'x', 'core'), split_axis=0, concat_axis=0, til...  20.1 us
    all_to_all x1, blocking collectives, shards(): lax.all_to_all(send.reshape(COLUMNS * HELPERS, lines, LANES), ('x', 'core...  19.7 us
    dot_general x1, matrix products, shards(): projected = jnp.dot(embeds, head_rows, preferred_element_type=F32)  1.76 us
    unnamed x10, local copies, waits for them, and re-layouts  1.59 us

profile of v4, /device:TPU:1, one launch (start us, length us, event | category | flops | bytes accessed | tf_op | source)
XLA Modules:
  0.0 72.8 jit_solution(8417683355601582634)
XLA Ops:
  0.6 0.0 copy-start
  0.6 0.0 copy-start.3
  0.7 0.0 copy-start.2
  0.7 1.6 %copy-done = bf16[4096,256]{1,0:T(8,128)(2,1)S(1)} copy-done((bf16[4096,256]{1,0:T(8,128)(2,1)S(1)}, bf16[4096,256]{1,0:T(8,128)(2,1)}, u32[]{:S(2)}) %copy-start) | copy-done | bytes 2097176
  2.2 0.0 copy-start.4
  2.2 1.8 %multiply_reduce_fusion = (f32[128]{0:T(128)S(1)}, f32[128,256]{1,0:T(8,128)S(1)}) fusion(bf16[128,4096]{1,0:T(8,128)(2,1)} %param.5, bf16[4096,256]{1,0:T(8,128)(2,1)S(1)} %copy-done), kind=kOutput, calls=%fused_computation.1 | convolution fusion | flops 268500864 | bytes 3277312 | tf_op jit(solution)/shard_map/dot_general | solution.py:160
  4.0 0.1 multiply_convert_fusion.prefix_ref
  4.1 0.0 copy-start.1
  4.1 0.0 copy-done.3
  4.1 0.0 copy-done.2
  4.1 0.0 copy-done.4
  4.1 0.5 scatter.1
  4.7 26.1 %all_to_all.21.got_ref = bf16[16,9,4,128]{3,2,1,0:T(4,128)(2,1)S(1)} all-to-all(bf16[16,9,4,128]{3,2,1,0:T(4,128)(2,1)S(1)} %get-tuple-element.4), channel_id=1, replica_groups={{256,288,320,352,384,416,448,480,0,32,64,96,128,160,192,224},{257,289,3..., dimensions={0} | all-to-all | bytes 294912 | tf_op jit(solution)/shard_map/all_to_all | solution.py:175
  30.8 0.3 sort.1
  31.1 19.7 %all_to_all.22 = bf16[32,72,128]{2,1,0:T(8,128)(2,1)S(1)} all-to-all(bf16[32,72,128]{2,1,0:T(8,128)(2,1)S(1)} %bitcast.12), channel_id=1, replica_groups=mesh['z'=16,'x'=4,'core'=2,'help'=4] {'x','core','help'}, dimensions={0} | all-to-all | bytes 1179648 | tf_op jit(solution)/shard_map/all_to_all | solution.py:187
  50.8 1.2 %best.1 = f32[128,128]{1,0:T(8,128)S(1)} custom-call(bf16[8,4,72,128]{3,2,1,0:T(8,128)(2,1)S(1)} %bitcast.13), custom_call_target="tpu_custom_call" | custom-call | tf_op jit(solution)/shard_map/best/pallas_call | solution.py:194
  52.0 20.1 %all_to_all.23 = f32[128,1,128]{2,1,0:T(1,128)S(1)} all-to-all(f32[128,1,128]{2,1,0:T(1,128)S(1)} %bitcast.14), channel_id=1, replica_groups={{272,276,280,284,256,260,264,268,304,308,312,316,288,292,296,300,336,34..., dimensions={0} | all-to-all | bytes 131072 | tf_op jit(solution)/shard_map/all_to_all | solution.py:204
  72.1 0.6 finish.1
  72.8 0.0 copy-done.1
  (1 shorter events, 0.0 us)
Async XLA Ops:
  0.6 1.6 %copy-start = (bf16[4096,256]{1,0:T(8,128)(2,1)S(1)}, bf16[4096,256]{1,0:T(8,128)(2,1)}, u32[]{:S(2)}) copy-start(bf16[4096,256]{1,0:T(8,128)(2,1)} %param.6) | copy-start | bytes 6291460
  0.6 3.5 %copy-start.3 = (s32[128]{0:T(128)S(1)}, s32[128]{0:T(128)}, u32[]{:S(2)}) copy-start(s32[128]{0:T(128)} %param.9) | copy-start | bytes 1540
  0.7 3.5 %copy-start.2 = (s32[2048]{0:T(1024)S(1)}, s32[2048]{0:T(1024)}, u32[]{:S(2)}) copy-start(s32[2048]{0:T(1024)} %param.8) | copy-start | bytes 24580
  2.2 1.9 %copy-start.4 = (s32[128]{0:T(128)S(1)}, s32[128]{0:T(128)}, u32[]{:S(2)}) copy-start(s32[128]{0:T(128)} %param.7) | copy-start | bytes 1540
  4.1 68.6 %copy-start.1 = (bf16[128,256]{1,0:T(8,128)(2,1)}, bf16[128,256]{1,0:T(8,128)(2,1)S(1)}, u32[]{:S(2)}) copy-start(bf16[128,256]{1,0:T(8,128)(2,1)S(1)} %multiply_convert_fusion.prefix_ref) | copy-start | bytes 196612

commit v5 on v4

--- a/solution.py
+++ b/solution.py
@@ -38,11 +38,11 @@
     return jnp.dot(left, right, preferred_element_type=F32)
 
 
-def scatter_kernel(prefix_ref, cluster_ref, owner_ref, live_ref, send_ref, target_ref):
+def index_kernel(packed_ref, target_ref, hit_ref, label_ref):
     square = (LANES, LANES)
-    cluster = cluster_ref[...]
+    cluster = packed_ref[16:17]
     high, low = cluster >> 7, cluster & 127
-    by_low = dot(owner_ref[...].astype(F32).astype(BF16), hot(iota(square, 0) == low))
+    by_low = dot(packed_ref[:16].astype(F32).astype(BF16), hot(iota(square, 0) == low))
     owner = jnp.sum(jnp.where(iota(by_low.shape, 0) == high, by_low, 0.0), axis=0, keepdims=True)
     owner = owner.astype(jnp.int32)
     owner_hot = hot(iota(square, 0) == owner)
@@ -54,20 +54,23 @@
     target = target ^ (PLANE_TURN * PLANE_SLOTS)
     target_ref[...] = jnp.broadcast_to(target ^ (COLUMN_TURN * SLOTS), target_ref.shape)
 
-    live = live_ref[...] == 1
+    live = packed_ref[17:18] == 1
     high_label = jnp.where(live, high + 1, 0)
     low_label = jnp.where(live, low, 0)
     line = iota(square, 0)
     part = jnp.where((line & 7) == 0, high_label, jnp.where((line & 7) == 1, low_label, 0))
     part = jnp.where((line >> 3) == (target >> 4), part, 0).astype(F32).astype(BF16)
-    labels = dot_nt(part, hot(line == (target & 15))).reshape(PLANES, 8, LANES)
-
-    rows = dot(hot(iota((SLAB, LANES), 0) == target), prefix_ref[...])
-    rows = rows.reshape(PLANES, PLANE_SLOTS, 2 * LANES)
+    label_ref[...] = dot_nt(part, hot(line == (target & 15)))
+    hit_ref[...] = hot(iota((SLAB, LANES), 0) == target)
+
+
+def scatter_kernel(prefix_ref, hit_ref, label_ref, send_ref):
+    rows = dot(hit_ref[...], prefix_ref[...]).reshape(PLANES, PLANE_SLOTS, 2 * LANES)
     rows = jnp.concatenate([rows[:, :, :LANES], rows[:, :, LANES:]], axis=1)
     rows = rows.reshape(PLANES, PIECES, 8, LANES)
+    labels = label_ref[...].reshape(PLANES, 1, 8, LANES)
     send_ref[...] = jnp.concatenate(
-        [rows[:, :, :4], rows[:, :, 4:], labels[:, :4].reshape(PLANES, 1, 4, LANES)], axis=1
+        [rows[:, :, :4], rows[:, :, 4:], labels[:, :, :4]], axis=1
     ).astype(BF16)
 
 
@@ -157,20 +160,32 @@
 def shards(embeds, head_rows, cluster_of, owner_of, live_mask):
     row_count = embeds.shape[0]
     live = live_mask.reshape(1, row_count)
+    packed = jnp.concatenate([owner_of, cluster_of, live_mask]).reshape(-1, LANES)
+    target, hit, label = pl.pallas_call(
+        index_kernel,
+        out_shape=(
+            jax.ShapeDtypeStruct((8, row_count), jnp.int32),
+            jax.ShapeDtypeStruct((SLAB, row_count), BF16),
+            jax.ShapeDtypeStruct((PLANES * 8, LANES), F32),
+        ),
+        in_specs=[VMEM],
+        out_specs=(VMEM,) * 3,
+        compiler_params=LIMIT,
+        cost_estimate=pl.CostEstimate(flops=8_000_000_000, bytes_accessed=0, transcendentals=0),
+        name="index",
+    )(packed)
+    embeds, hit = lax.optimization_barrier((embeds, hit))
     projected = jnp.dot(embeds, head_rows, preferred_element_type=F32)
     norm = lax.rsqrt(jnp.sum(projected * projected, axis=1, keepdims=True) + NORM_EPS)
     prefix = (projected * norm).astype(BF16)
-    send, target = pl.pallas_call(
+    send = pl.pallas_call(
         scatter_kernel,
-        out_shape=(
-            jax.ShapeDtypeStruct((PLANES, 2 * PIECES + 1, 4, LANES), BF16),
-            jax.ShapeDtypeStruct((8, row_count), jnp.int32),
-        ),
-        in_specs=[VMEM] * 4,
-        out_specs=(VMEM, VMEM),
+        out_shape=jax.ShapeDtypeStruct((PLANES, 2 * PIECES + 1, 4, LANES), BF16),
+        in_specs=[VMEM] * 3,
+        out_specs=VMEM,
         compiler_params=LIMIT,
         name="scatter",
-    )(prefix, cluster_of.reshape(1, row_count), owner_of.reshape(-1, LANES), live)
+    )(prefix, hit, label)
     planes = [[spot ^ PLANE_TURN for spot in range(PLANES)]]
     got = lax.all_to_all(
         send, "z", split_axis=0, concat_axis=0, tiled=True, axis_index_groups=planes

time: 73 us -> 72.1 us (0.988)
  matrix products: 1.76 us -> 0.54 us
  other arithmetic: 0.1 us -> 0.97 us
    dot_general x1, matrix products: 1.76 us -> 0.54 us  [shards(): projected = jnp.dot(embeds, head_rows, preferred_element_type=F32)]
    reshape x0 -> x1, other arithmetic: none -> 0.88 us  [shards(): jnp.concatenate([owner_of, cluster_of, live_mask]).reshape(-1, LANES)]
    unnamed x10 -> x8, local copies, waits for them, and re-layouts: 1.59 us -> 0.88 us
where the time goes in v5:
time: 72.1 us; the launch traced here: 71.8 us
  blocking collectives  65.9 us (91%)
  Pallas kernels  2.84 us (4%)
  other arithmetic  0.97 us (1%)
  local copies, waits for them, and re-layouts  0.88 us (1%)
    all_to_all x1, blocking collectives, shards(): lax.all_to_all(send, 'z', split_axis=0, concat_axis=0, tiled=True, axis_i...  26.1 us
    all_to_all x1, blocking collectives, shards(): lax.all_to_all(best, ('z', 'x', 'core'), split_axis=0, concat_axis=0, til...  20.1 us
    all_to_all x1, blocking collectives, shards(): lax.all_to_all(send.reshape(COLUMNS * HELPERS, lines, LANES), ('x', 'core...  19.7 us

profile of v5, /device:TPU:1, one launch (start us, length us, event | category | flops | bytes accessed | tf_op | source)
XLA Modules:
  0.0 71.8 jit_solution(17256165489285187245)
XLA Ops:
  0.6 0.0 copy-start
  0.6 0.9 %add_bitcast_fusion.packed_ref = s32[18,128]{1,0:T(8,128)S(1)} fusion(s32[128]{0:T(128)} %param.9, s32[128]{0:T(128)} %param.7, s32[2048]{0:T(1024)} %param.8), kind=kLoop, calls=%fused_computation.2 | loop fusion | flops 4608 | bytes 18432 | tf_op jit(solution)/shard_map/reshape | solution.py:163
  1.5 0.0 copy-start.3
  1.5 0.5 index.1
  2.1 0.2 copy-done
  2.3 0.6 copy-done.3
  2.9 0.5 multiply_reduce_fusion
  3.5 0.0 copy-start.2
  3.5 0.1 multiply_convert_fusion.prefix_ref
  3.6 0.0 copy-start.1
  3.6 0.2 scatter.1
  3.8 26.1 %all_to_all.21.got_ref = bf16[16,9,4,128]{3,2,1,0:T(4,128)(2,1)S(1)} all-to-all(bf16[16,9,4,128]{3,2,1,0:T(4,128)(2,1)S(1)} %scatter.1), channel_id=1, replica_groups={{256,288,320,352,384,416,448,480,0,32,64,96,128,160,192,224},{257,289,3..., dimensions={0} | all-to-all | bytes 294912 | tf_op jit(solution)/shard_map/all_to_all | solution.py:190
  29.9 0.3 sort.1
  30.2 19.7 %all_to_all.22 = bf16[32,72,128]{2,1,0:T(8,128)(2,1)S(1)} all-to-all(bf16[32,72,128]{2,1,0:T(8,128)(2,1)S(1)} %bitcast.12), channel_id=1, replica_groups=mesh['z'=16,'x'=4,'core'=2,'help'=4] {'x','core','help'}, dimensions={0} | all-to-all | bytes 1179648 | tf_op jit(solution)/shard_map/all_to_all | solution.py:202
  49.9 1.2 %best.1 = f32[128,128]{1,0:T(8,128)S(1)} custom-call(bf16[8,4,72,128]{3,2,1,0:T(8,128)(2,1)S(1)} %bitcast.13), custom_call_target="tpu_custom_call" | custom-call | tf_op jit(solution)/shard_map/best/pallas_call | solution.py:209
  51.1 20.1 %all_to_all.23 = f32[128,1,128]{2,1,0:T(1,128)S(1)} all-to-all(f32[128,1,128]{2,1,0:T(1,128)S(1)} %bitcast.14), channel_id=1, replica_groups={{272,276,280,284,256,260,264,268,304,308,312,316,288,292,296,300,336,34..., dimensions={0} | all-to-all | bytes 131072 | tf_op jit(solution)/shard_map/all_to_all | solution.py:219
  71.2 0.0 copy-done.2
  71.2 0.6 finish.1
  71.8 0.0 copy-done.1
  (1 shorter events, 0.0 us)
Async XLA Ops:
  0.6 1.6 %copy-start = (bf16[4096,256]{1,0:T(8,128)(2,1)S(1)}, bf16[4096,256]{1,0:T(8,128)(2,1)}, u32[]{:S(2)}) copy-start(bf16[4096,256]{1,0:T(8,128)(2,1)} %param.6) | copy-start | bytes 6291460
  1.5 1.4 %copy-start.3 = (bf16[128,4096]{1,0:T(8,128)(2,1)S(1)}, bf16[128,4096]{1,0:T(8,128)(2,1)}, u32[]{:S(2)}) copy-start(bf16[128,4096]{1,0:T(8,128)(2,1)} %param.5) | copy-start | bytes 3145732
  3.5 67.8 %copy-start.2 = (s32[128]{0:T(128)S(1)}, s32[128]{0:T(128)}, u32[]{:S(2)}) copy-start(s32[128]{0:T(128)} %param.9) | copy-start | bytes 1540
  3.6 68.3 %copy-start.1 = (bf16[128,256]{1,0:T(8,128)(2,1)}, bf16[128,256]{1,0:T(8,128)(2,1)S(1)}, u32[]{:S(2)}) copy-start(bf16[128,256]{1,0:T(8,128)(2,1)S(1)} %multiply_convert_fusion.prefix_ref) | copy-start | bytes 196612

commit v6 on v5

--- a/solution.py
+++ b/solution.py
@@ -15,6 +15,7 @@
 SLAB = PLANES * PLANE_SLOTS
 OWNER_SLOTS = PLANES * SLOTS
 PIECES = 2 * PLANE_SLOTS // 8
+PLANE_FIRST = 11
 PLANE_TURN = 8
 COLUMN_TURN = 4
 
@@ -51,8 +52,9 @@
     )
     slot = jnp.sum(jnp.where(iota(square, 0) < iota(square, 1), same, 0.0), axis=0, keepdims=True)
     target = owner * SLOTS + slot.astype(jnp.int32)
-    target = target ^ (PLANE_TURN * PLANE_SLOTS)
-    target_ref[...] = jnp.broadcast_to(target ^ (COLUMN_TURN * SLOTS), target_ref.shape)
+    back = target ^ (PLANE_TURN * PLANE_SLOTS + COLUMN_TURN * SLOTS)
+    target_ref[...] = jnp.broadcast_to(back, target_ref.shape)
+    target = (target - PLANE_FIRST * PLANE_SLOTS) & (SLAB - 1)
 
     live = packed_ref[17:18] == 1
     high_label = jnp.where(live, high + 1, 0)
@@ -101,6 +103,10 @@
         send_ref[:, helper] = out
 
 
+def from_first(plane_back):
+    return (plane_back + PLANE_TURN - PLANE_FIRST) & (PLANES - 1)
+
+
 def best_kernel(got_ref, out_ref):
     helper = lax.axis_index("help")
     sources = COLUMNS * HELPERS
@@ -112,7 +118,7 @@
     own_high = got_ref[:, helper, OWNER_SLOTS : 2 * OWNER_SLOTS].reshape(SLAB, LANES)
 
     dest = iota((SLAB, SLAB), 0)
-    in_owner = ((dest >> 3) & 15) * SLOTS + (dest >> 7)
+    in_owner = from_first(dest >> 3) * SLOTS + (dest >> 7)
     order = hot(iota((SLAB, SLAB), 1) == ((dest & 7) ^ COLUMN_TURN) * OWNER_SLOTS + in_owner)
     own = dot(order, jnp.concatenate([own_low, own_high], axis=1)).astype(BF16)
     scores = dot_nt(own, columns)
@@ -128,7 +134,7 @@
     line = iota(shape, 0)
     own_spread = dot(hot(iota(shape, 1) == (((line & 7) ^ COLUMN_TURN) * HELPERS + helper) * 8), tiles)
     line, lane = iota((SLAB, LANES), 0), iota((SLAB, LANES), 1)
-    line = ((line >> 3) & 15) * SLOTS + (line >> 7)
+    line = from_first(line >> 3) * SLOTS + (line >> 7)
     own_label = jnp.sum(
         jnp.where(lane == line, own_spread * 128.0, jnp.where(lane == line + 32, own_spread, 0.0)),
         axis=1,
@@ -136,7 +142,7 @@
     )
     own_label = jnp.where(own_label > 0.5, own_label, -1.0)
     line = iota((SLAB, 1), 0)
-    own_index = (((line & 7) ^ COLUMN_TURN) * HELPERS + helper) * OWNER_SLOTS + ((line >> 3) & 15) * SLOTS + (line >> 7)
+    own_index = (((line & 7) ^ COLUMN_TURN) * HELPERS + helper) * OWNER_SLOTS + from_first(line >> 3) * SLOTS + (line >> 7)
     allowed = (own_label == column_label) & (own_index != iota((SLAB, total), 1))
     best = jnp.max(jnp.where(allowed, scores, -1.0), axis=1, keepdims=True)
     half = SLAB // 2
@@ -186,7 +192,7 @@
         compiler_params=LIMIT,
         name="scatter",
     )(prefix, hit, label)
-    planes = [[spot ^ PLANE_TURN for spot in range(PLANES)]]
+    planes = [[(spot + PLANE_FIRST) % PLANES for spot in range(PLANES)]]
     got = lax.all_to_all(
         send, "z", split_axis=0, concat_axis=0, tiled=True, axis_index_groups=planes
     )

time: 72.1 us -> 72 us (level)
    all_to_all x1, blocking collectives: 26.1 us -> 25.3 us  [shards(): lax.all_to_all(send, 'z', split_axis=0, concat_axis=0, tiled=True, axis_i...]
where the time goes in v6:
time: 72 us; the launch traced here: 71.7 us
  blocking collectives  65.8 us (91%)
  Pallas kernels  2.85 us (4%)
  other arithmetic  0.97 us (1%)
  local copies, waits for them, and re-layouts  0.88 us (1%)
    all_to_all x1, blocking collectives, shards(): lax.all_to_all(send, 'z', split_axis=0, concat_axis=0, tiled=True, axis_i...  25.3 us
    all_to_all x1, blocking collectives, shards(): lax.all_to_all(send.reshape(COLUMNS * HELPERS, lines, LANES), ('x', 'core...  20.4 us
    all_to_all x1, blocking collectives, shards(): lax.all_to_all(best, ('z', 'x', 'core'), split_axis=0, concat_axis=0, til...  20.1 us

profile of v6, /device:TPU:1, one launch (start us, length us, event | category | flops | bytes accessed | tf_op | source)
XLA Modules:
  0.0 71.7 jit_solution(3388069431121391271)
XLA Ops:
  0.6 0.0 copy-start
  0.6 0.9 %add_bitcast_fusion.packed_ref = s32[18,128]{1,0:T(8,128)S(1)} fusion(s32[128]{0:T(128)} %param.9, s32[128]{0:T(128)} %param.7, s32[2048]{0:T(1024)} %param.8), kind=kLoop, calls=%fused_computation.2 | loop fusion | flops 4608 | bytes 18432 | tf_op jit(solution)/shard_map/reshape | solution.py:169
  1.5 0.0 copy-start.3
  1.5 0.5 index.1
  2.1 0.2 copy-done
  2.3 0.6 copy-done.3
  2.9 0.5 multiply_reduce_fusion
  3.5 0.0 copy-start.2
  3.5 0.1 multiply_convert_fusion.prefix_ref
  3.6 0.0 copy-start.1
  3.6 0.2 scatter.1
  3.8 25.3 %all_to_all.21.got_ref = bf16[16,9,4,128]{3,2,1,0:T(4,128)(2,1)S(1)} all-to-all(bf16[16,9,4,128]{3,2,1,0:T(4,128)(2,1)S(1)} %scatter.1), channel_id=1, replica_groups={{352,384,416,448,480,0,32,64,96,128,160,192,224,256,288,320},{353,385,4..., dimensions={0} | all-to-all | bytes 294912 | tf_op jit(solution)/shard_map/all_to_all | solution.py:196
  29.1 0.3 sort.1
  29.4 20.4 %all_to_all.22 = bf16[32,72,128]{2,1,0:T(8,128)(2,1)S(1)} all-to-all(bf16[32,72,128]{2,1,0:T(8,128)(2,1)S(1)} %bitcast.12), channel_id=1, replica_groups=mesh['z'=16,'x'=4,'core'=2,'help'=4] {'x','core','help'}, dimensions={0} | all-to-all | bytes 1179648 | tf_op jit(solution)/shard_map/all_to_all | solution.py:208
  49.8 1.2 %best.1 = f32[128,128]{1,0:T(8,128)S(1)} custom-call(bf16[8,4,72,128]{3,2,1,0:T(8,128)(2,1)S(1)} %bitcast.13), custom_call_target="tpu_custom_call" | custom-call | tf_op jit(solution)/shard_map/best/pallas_call | solution.py:215
  51.0 20.1 %all_to_all.23 = f32[128,1,128]{2,1,0:T(1,128)S(1)} all-to-all(f32[128,1,128]{2,1,0:T(1,128)S(1)} %bitcast.14), channel_id=1, replica_groups={{272,276,280,284,256,260,264,268,304,308,312,316,288,292,296,300,336,34..., dimensions={0} | all-to-all | bytes 131072 | tf_op jit(solution)/shard_map/all_to_all | solution.py:225
  71.1 0.0 copy-done.2
  71.1 0.6 finish.1
  71.7 0.0 copy-done.1
  (1 shorter events, 0.0 us)
Async XLA Ops:
  0.6 1.6 %copy-start = (bf16[4096,256]{1,0:T(8,128)(2,1)S(1)}, bf16[4096,256]{1,0:T(8,128)(2,1)}, u32[]{:S(2)}) copy-start(bf16[4096,256]{1,0:T(8,128)(2,1)} %param.6) | copy-start | bytes 6291460
  1.5 1.4 %copy-start.3 = (bf16[128,4096]{1,0:T(8,128)(2,1)S(1)}, bf16[128,4096]{1,0:T(8,128)(2,1)}, u32[]{:S(2)}) copy-start(bf16[128,4096]{1,0:T(8,128)(2,1)} %param.5) | copy-start | bytes 3145732
  3.5 67.7 %copy-start.2 = (s32[128]{0:T(128)S(1)}, s32[128]{0:T(128)}, u32[]{:S(2)}) copy-start(s32[128]{0:T(128)} %param.9) | copy-start | bytes 1540
  3.6 68.2 %copy-start.1 = (bf16[128,256]{1,0:T(8,128)(2,1)}, bf16[128,256]{1,0:T(8,128)(2,1)S(1)}, u32[]{:S(2)}) copy-start(bf16[128,256]{1,0:T(8,128)(2,1)S(1)} %multiply_convert_fusion.prefix_ref) | copy-start | bytes 196612

commit v7 on v5

--- a/solution.py
+++ b/solution.py
@@ -52,7 +52,8 @@
     slot = jnp.sum(jnp.where(iota(square, 0) < iota(square, 1), same, 0.0), axis=0, keepdims=True)
     target = owner * SLOTS + slot.astype(jnp.int32)
     target = target ^ (PLANE_TURN * PLANE_SLOTS)
-    target_ref[...] = jnp.broadcast_to(target ^ (COLUMN_TURN * SLOTS), target_ref.shape)
+    back = (((target >> 1) & 7) ^ COLUMN_TURN) * OWNER_SLOTS + (target >> 4) * SLOTS + (target & 1)
+    target_ref[...] = jnp.broadcast_to(back, target_ref.shape)
 
     live = packed_ref[17:18] == 1
     high_label = jnp.where(live, high + 1, 0)
@@ -75,73 +76,70 @@
 
 
 def sort_kernel(got_ref, send_ref):
+    helper = lax.axis_index("help")
     pieces = got_ref[...].astype(F32)
     got = jnp.concatenate([pieces[:, :PIECES], pieces[:, PIECES : 2 * PIECES]], axis=2)
     got = got.reshape(PLANES, 2 * PLANE_SLOTS, LANES)
     low = got[:, :PLANE_SLOTS].reshape(SLAB, LANES).astype(BF16)
     high = got[:, PLANE_SLOTS:].reshape(SLAB, LANES).astype(BF16)
     dest = iota((SLAB, SLAB), 0)
-    source = ((dest >> 1) & 15) * PLANE_SLOTS + (dest >> 5) * SLOTS + (dest & 1)
+    source = (dest & 15) * PLANE_SLOTS + (dest >> 5) * SLOTS + ((dest >> 4) & 1)
     order = hot(iota((SLAB, SLAB), 1) == source)
     rows = dot(order, jnp.concatenate([low, high], axis=1))
     rows = rows.reshape(COLUMNS, OWNER_SLOTS, 2 * LANES)
 
-    square = (LANES, LANES)
     tiles = pieces[:, 2 * PIECES].reshape(PLANES, 4, LANES)
     tiles = jnp.concatenate([tiles, tiles], axis=1).reshape(PLANES * 8, LANES).astype(BF16)
-    line, lane = iota(square, 0), iota(square, 1)
-    pick = ((line & 31) >> 1) * 8 + (line >> 5)
-    spread = dot(hot((lane == pick) & (line < 2 * OWNER_SLOTS)), tiles)
-    spread = jnp.where((lane & 1) == (line & 1), spread, 0.0).astype(BF16)
+    line, lane = iota((2 * LANES, LANES), 0), iota((2 * LANES, LANES), 1)
+    mine = ((line >> 5) & 3) == helper
+    spread = dot(hot((lane == (line & 15) * 8 + (line >> 7)) & mine), tiles)
+    spread = jnp.where((lane & 1) == ((line >> 4) & 1), spread, 0.0).astype(BF16)
     group = (COLUMNS * 8, LANES)
     labels = dot_nt(hot((iota(group, 1) >> 1) == (iota(group, 0) >> 3)), spread)
+    labels = jnp.where((iota(group, 0) & 7) < 4, labels[:, :LANES], labels[:, LANES:])
     labels = labels.reshape(COLUMNS, 8, LANES)
     out = jnp.concatenate([rows[:, :, :LANES], rows[:, :, LANES:], labels], axis=1).astype(BF16)
     for helper in range(HELPERS):
         send_ref[:, helper] = out
 
 
+def turned(blocks):
+    return jnp.concatenate([blocks[COLUMN_TURN:], blocks[:COLUMN_TURN]], axis=0)
+
+
 def best_kernel(got_ref, out_ref):
     helper = lax.axis_index("help")
-    sources = COLUMNS * HELPERS
-    total = sources * OWNER_SLOTS
+    total = COLUMNS * HELPERS * OWNER_SLOTS
     low = got_ref[:, :, :OWNER_SLOTS].reshape(total, LANES)
     high = got_ref[:, :, OWNER_SLOTS : 2 * OWNER_SLOTS].reshape(total, LANES)
-    columns = jnp.concatenate([low, high], axis=1)
-    own_low = got_ref[:, helper, :OWNER_SLOTS].reshape(SLAB, LANES)
-    own_high = got_ref[:, helper, OWNER_SLOTS : 2 * OWNER_SLOTS].reshape(SLAB, LANES)
-
-    dest = iota((SLAB, SLAB), 0)
-    in_owner = ((dest >> 3) & 15) * SLOTS + (dest >> 7)
-    order = hot(iota((SLAB, SLAB), 1) == ((dest & 7) ^ COLUMN_TURN) * OWNER_SLOTS + in_owner)
-    own = dot(order, jnp.concatenate([own_low, own_high], axis=1)).astype(BF16)
-    scores = dot_nt(own, columns)
-
-    tiles = got_ref[...].astype(F32)[:, :, 2 * OWNER_SLOTS :].reshape(sources * 8, LANES).astype(BF16)
-    shape = (total, sources * 8)
-    spread = dot(hot(iota(shape, 1) == (iota(shape, 0) >> 5) * 8), tiles)
-    line, lane = iota((total, LANES), 0) & 31, iota((total, LANES), 1)
-    spread = jnp.where(lane == line, spread * 128.0, jnp.where(lane == line + 32, spread, 0.0))
-    column_label = dot_nt(jnp.ones((8, LANES), BF16), spread.astype(BF16))[:1]
-
-    shape = (SLAB, sources * 8)
-    line = iota(shape, 0)
-    own_spread = dot(hot(iota(shape, 1) == (((line & 7) ^ COLUMN_TURN) * HELPERS + helper) * 8), tiles)
-    line, lane = iota((SLAB, LANES), 0), iota((SLAB, LANES), 1)
-    line = ((line >> 3) & 15) * SLOTS + (line >> 7)
-    own_label = jnp.sum(
-        jnp.where(lane == line, own_spread * 128.0, jnp.where(lane == line + 32, own_spread, 0.0)),
-        axis=1,
-        keepdims=True,
-    )
+
+    own = got_ref[:, helper, : 2 * OWNER_SLOTS].reshape(COLUMNS, 2 * SLOTS, PLANES, LANES)
+    own = turned(own)
+    parts = [own[:, part].reshape(COLUMNS * PLANES, LANES) for part in range(2 * SLOTS)]
+    own = jnp.concatenate(
+        [jnp.concatenate(parts[:SLOTS], axis=0), jnp.concatenate(parts[SLOTS:], axis=0)], axis=1
+    )
+    scores = dot_nt(own, jnp.concatenate([low, high], axis=1))
+
+    label = jnp.sum(got_ref[...].astype(F32)[:, :, 2 * OWNER_SLOTS :], axis=1)
+    label = label[:, 0:1] * 128.0 + label[:, 4:5]
+    shape = (SLOTS, COLUMNS, PLANES, LANES)
+    small = (SLOTS, 1, PLANES, LANES)
+    self_lane = iota(small, 3) == helper * OWNER_SLOTS + iota(small, 0) * PLANES + iota(small, 2)
+    spread = jnp.where(self_lane, turned(label)[None], 0.0)
+    own_label = jnp.sum(spread, axis=3, keepdims=True)
     own_label = jnp.where(own_label > 0.5, own_label, -1.0)
-    line = iota((SLAB, 1), 0)
-    own_index = (((line & 7) ^ COLUMN_TURN) * HELPERS + helper) * OWNER_SLOTS + ((line >> 3) & 15) * SLOTS + (line >> 7)
-    allowed = (own_label == column_label) & (own_index != iota((SLAB, total), 1))
-    best = jnp.max(jnp.where(allowed, scores, -1.0), axis=1, keepdims=True)
-    half = SLAB // 2
+    best = jnp.full(shape, -1.0, F32)
+    for column in range(COLUMNS):
+        block = scores[:, column * LANES : (column + 1) * LANES].reshape(shape)
+        block = jnp.where(own_label == label[column][None, None], block, -1.0)
+        back = column ^ COLUMN_TURN
+        no_self = jnp.where(self_lane, -1.0, block[:, back : back + 1])
+        parts = [block[:, :back], no_self, block[:, back + 1 :]]
+        best = jnp.maximum(best, jnp.concatenate([p for p in parts if p.shape[1]], axis=1))
+    best = jnp.max(best, axis=3, keepdims=True).reshape(SLOTS, COLUMNS * PLANES, 1)
     lane = iota(out_ref.shape, 1)
-    out_ref[...] = jnp.where(lane == 0, best[:half], jnp.where(lane == 1, best[half:], 0.0))
+    out_ref[...] = jnp.where(lane == 0, best[0], jnp.where(lane == 1, best[1], 0.0))
 
 
 def finish_kernel(got_ref, target_ref, live_ref, out_ref):
@@ -171,7 +169,7 @@
         in_specs=[VMEM],
         out_specs=(VMEM,) * 3,
         compiler_params=LIMIT,
-        cost_estimate=pl.CostEstimate(flops=8_000_000_000, bytes_accessed=0, transcendentals=0),
+        cost_estimate=pl.CostEstimate(flops=700_000_000, bytes_accessed=0, transcendentals=0),
         name="index",
     )(packed)
     embeds, hit = lax.optimization_barrier((embeds, hit))
@@ -214,8 +212,12 @@
         compiler_params=LIMIT,
         name="best",
     )(got.reshape(COLUMNS, HELPERS, lines, LANES))
-    turn = PLANE_TURN * COLUMNS + COLUMN_TURN
-    owners = [[spot ^ turn for spot in range(PLANES * COLUMNS)]]
+    owners = [
+        [
+            (spot % PLANES ^ PLANE_TURN) * COLUMNS + (spot // PLANES ^ COLUMN_TURN)
+            for spot in range(PLANES * COLUMNS)
+        ]
+    ]
     back = lax.all_to_all(
         best, ("z", "x", "core"), split_axis=0, concat_axis=0, tiled=True, axis_index_groups=owners
     )

time: 72.1 us -> 70.9 us (0.983)
  Pallas kernels: 2.84 us -> 2.04 us
    pallas_call x1, Pallas kernels: 1.24 us -> 0.41 us  [shards(): pl.pallas_call(best_kernel, out_shape=jax.ShapeDtypeStruct((PLANES * COLU...]
where the time goes in v7:
time: 70.9 us; the launch traced here: 70.6 us
  blocking collectives  65.8 us (93%)
  Pallas kernels  2.04 us (3%)
  other arithmetic  0.98 us (1%)
  between operations  0.71 us (1%)
    all_to_all x1, blocking collectives, shards(): lax.all_to_all(send, 'z', split_axis=0, concat_axis=0, tiled=True, axis_i...  26.1 us
    all_to_all x1, blocking collectives, shards(): lax.all_to_all(best, ('z', 'x', 'core'), split_axis=0, concat_axis=0, til...  20 us
    all_to_all x1, blocking collectives, shards(): lax.all_to_all(send.reshape(COLUMNS * HELPERS, lines, LANES), ('x', 'core...  19.7 us

profile of v7, /device:TPU:1, one launch (start us, length us, event | category | flops | bytes accessed | tf_op | source)
XLA Modules:
  0.0 70.6 jit_solution(17424482609710770740)
XLA Ops:
  0.6 0.0 copy-start
  0.6 0.0 copy-start.3
  0.7 0.9 %add_bitcast_fusion.packed_ref = s32[18,128]{1,0:T(8,128)S(1)} fusion(s32[128]{0:T(128)} %param.9, s32[128]{0:T(128)} %param.7, s32[2048]{0:T(1024)} %param.8), kind=kLoop, calls=%fused_computation.2 | loop fusion | flops 4608 | bytes 18432 | tf_op jit(solution)/shard_map/reshape | solution.py:161
  1.5 0.5 index.1
  2.1 0.2 copy-done
  2.3 0.3 copy-done.3
  2.5 0.5 multiply_reduce_fusion
  3.1 0.0 copy-start.2
  3.1 0.1 multiply_convert_fusion.prefix_ref
  3.2 0.0 copy-start.1
  3.2 0.2 scatter.1
  3.4 26.1 %all_to_all.21.got_ref = bf16[16,9,4,128]{3,2,1,0:T(4,128)(2,1)S(1)} all-to-all(bf16[16,9,4,128]{3,2,1,0:T(4,128)(2,1)S(1)} %scatter.1), channel_id=1, replica_groups={{256,288,320,352,384,416,448,480,0,32,64,96,128,160,192,224},{257,289,3..., dimensions={0} | all-to-all | bytes 294912 | tf_op jit(solution)/shard_map/all_to_all | solution.py:188
  29.5 0.3 sort.1
  29.8 19.7 %all_to_all.22 = bf16[32,72,128]{2,1,0:T(8,128)(2,1)S(1)} all-to-all(bf16[32,72,128]{2,1,0:T(8,128)(2,1)S(1)} %bitcast.12), channel_id=1, replica_groups=mesh['z'=16,'x'=4,'core'=2,'help'=4] {'x','core','help'}, dimensions={0} | all-to-all | bytes 1179648 | tf_op jit(solution)/shard_map/all_to_all | solution.py:200
  49.5 0.4 best.1
  49.9 20.0 %all_to_all.23 = f32[128,1,128]{2,1,0:T(1,128)S(1)} all-to-all(f32[128,1,128]{2,1,0:T(1,128)S(1)} %bitcast.14), channel_id=1, replica_groups={{272,304,336,368,400,432,464,496,16,48,80,112,144,176,208,240,276,308,3..., dimensions={0} | all-to-all | bytes 131072 | tf_op jit(solution)/shard_map/all_to_all | solution.py:221
  70.0 0.0 copy-done.2
  70.0 0.6 finish.1
  70.6 0.0 copy-done.1
  (1 shorter events, 0.0 us)
Async XLA Ops:
  0.6 1.6 %copy-start = (bf16[4096,256]{1,0:T(8,128)(2,1)S(1)}, bf16[4096,256]{1,0:T(8,128)(2,1)}, u32[]{:S(2)}) copy-start(bf16[4096,256]{1,0:T(8,128)(2,1)} %param.6) | copy-start | bytes 6291460
  0.6 1.9 %copy-start.3 = (bf16[128,4096]{1,0:T(8,128)(2,1)S(1)}, bf16[128,4096]{1,0:T(8,128)(2,1)}, u32[]{:S(2)}) copy-start(bf16[128,4096]{1,0:T(8,128)(2,1)} %param.5) | copy-start | bytes 3145732
  3.1 66.9 %copy-start.2 = (s32[128]{0:T(128)S(1)}, s32[128]{0:T(128)}, u32[]{:S(2)}) copy-start(s32[128]{0:T(128)} %param.9) | copy-start | bytes 1540
  3.2 67.4 %copy-start.1 = (bf16[128,256]{1,0:T(8,128)(2,1)}, bf16[128,256]{1,0:T(8,128)(2,1)S(1)}, u32[]{:S(2)}) copy-start(bf16[128,256]{1,0:T(8,128)(2,1)S(1)} %multiply_convert_fusion.prefix_ref) | copy-start | bytes 196612

commit v8 on v7

--- a/solution.py
+++ b/solution.py
@@ -16,7 +16,8 @@
 OWNER_SLOTS = PLANES * SLOTS
 PIECES = 2 * PLANE_SLOTS // 8
 PLANE_TURN = 8
-COLUMN_TURN = 4
+COLUMN_TURN = 5
+HELPER_TURN = 2
 
 F32 = jnp.float32
 BF16 = jnp.bfloat16
@@ -76,14 +77,14 @@
 
 
 def sort_kernel(got_ref, send_ref):
-    helper = lax.axis_index("help")
+    helper = lax.axis_index("help") ^ HELPER_TURN
     pieces = got_ref[...].astype(F32)
     got = jnp.concatenate([pieces[:, :PIECES], pieces[:, PIECES : 2 * PIECES]], axis=2)
     got = got.reshape(PLANES, 2 * PLANE_SLOTS, LANES)
     low = got[:, :PLANE_SLOTS].reshape(SLAB, LANES).astype(BF16)
     high = got[:, PLANE_SLOTS:].reshape(SLAB, LANES).astype(BF16)
     dest = iota((SLAB, SLAB), 0)
-    source = (dest & 15) * PLANE_SLOTS + (dest >> 5) * SLOTS + ((dest >> 4) & 1)
+    source = (dest & 15) * PLANE_SLOTS + ((dest >> 5) ^ COLUMN_TURN) * SLOTS + ((dest >> 4) & 1)
     order = hot(iota((SLAB, SLAB), 1) == source)
     rows = dot(order, jnp.concatenate([low, high], axis=1))
     rows = rows.reshape(COLUMNS, OWNER_SLOTS, 2 * LANES)
@@ -95,7 +96,7 @@
     spread = dot(hot((lane == (line & 15) * 8 + (line >> 7)) & mine), tiles)
     spread = jnp.where((lane & 1) == ((line >> 4) & 1), spread, 0.0).astype(BF16)
     group = (COLUMNS * 8, LANES)
-    labels = dot_nt(hot((iota(group, 1) >> 1) == (iota(group, 0) >> 3)), spread)
+    labels = dot_nt(hot((iota(group, 1) >> 1) == ((iota(group, 0) >> 3) ^ COLUMN_TURN)), spread)
     labels = jnp.where((iota(group, 0) & 7) < 4, labels[:, :LANES], labels[:, LANES:])
     labels = labels.reshape(COLUMNS, 8, LANES)
     out = jnp.concatenate([rows[:, :, :LANES], rows[:, :, LANES:], labels], axis=1).astype(BF16)
@@ -103,18 +104,13 @@
         send_ref[:, helper] = out
 
 
-def turned(blocks):
-    return jnp.concatenate([blocks[COLUMN_TURN:], blocks[:COLUMN_TURN]], axis=0)
-
-
 def best_kernel(got_ref, out_ref):
-    helper = lax.axis_index("help")
+    helper = lax.axis_index("help") ^ HELPER_TURN
     total = COLUMNS * HELPERS * OWNER_SLOTS
     low = got_ref[:, :, :OWNER_SLOTS].reshape(total, LANES)
     high = got_ref[:, :, OWNER_SLOTS : 2 * OWNER_SLOTS].reshape(total, LANES)
 
     own = got_ref[:, helper, : 2 * OWNER_SLOTS].reshape(COLUMNS, 2 * SLOTS, PLANES, LANES)
-    own = turned(own)
     parts = [own[:, part].reshape(COLUMNS * PLANES, LANES) for part in range(2 * SLOTS)]
     own = jnp.concatenate(
         [jnp.concatenate(parts[:SLOTS], axis=0), jnp.concatenate(parts[SLOTS:], axis=0)], axis=1
@@ -126,16 +122,15 @@
     shape = (SLOTS, COLUMNS, PLANES, LANES)
     small = (SLOTS, 1, PLANES, LANES)
     self_lane = iota(small, 3) == helper * OWNER_SLOTS + iota(small, 0) * PLANES + iota(small, 2)
-    spread = jnp.where(self_lane, turned(label)[None], 0.0)
+    spread = jnp.where(self_lane, label[None], 0.0)
     own_label = jnp.sum(spread, axis=3, keepdims=True)
     own_label = jnp.where(own_label > 0.5, own_label, -1.0)
     best = jnp.full(shape, -1.0, F32)
     for column in range(COLUMNS):
         block = scores[:, column * LANES : (column + 1) * LANES].reshape(shape)
         block = jnp.where(own_label == label[column][None, None], block, -1.0)
-        back = column ^ COLUMN_TURN
-        no_self = jnp.where(self_lane, -1.0, block[:, back : back + 1])
-        parts = [block[:, :back], no_self, block[:, back + 1 :]]
+        no_self = jnp.where(self_lane, -1.0, block[:, column : column + 1])
+        parts = [block[:, :column], no_self, block[:, column + 1 :]]
         best = jnp.maximum(best, jnp.concatenate([p for p in parts if p.shape[1]], axis=1))
     best = jnp.max(best, axis=3, keepdims=True).reshape(SLOTS, COLUMNS * PLANES, 1)
     lane = iota(out_ref.shape, 1)
@@ -197,12 +192,15 @@
         compiler_params=LIMIT,
         name="sort",
     )(got)
+    turn = COLUMN_TURN * HELPERS + HELPER_TURN
+    members = [[spot ^ turn for spot in range(COLUMNS * HELPERS)]]
     got = lax.all_to_all(
         send.reshape(COLUMNS * HELPERS, lines, LANES),
         ("x", "core", "help"),
         split_axis=0,
         concat_axis=0,
         tiled=True,
+        axis_index_groups=members,
     )
     best = pl.pallas_call(
         best_kernel,

time: 70.9 us -> 67.5 us (0.952)
  blocking collectives: 65.8 us -> 62.5 us
    all_to_all x1, blocking collectives: 19.7 us -> 16.9 us  [shards(): lax.all_to_all(send.reshape(COLUMNS * HELPERS, lines, LANES), ('x', 'core...]
where the time goes in v8:
time: 67.5 us; the launch traced here: 67.3 us
  blocking collectives  62.5 us (93%)
  Pallas kernels  2.04 us (3%)
  other arithmetic  0.98 us (1%)
  between operations  0.71 us (1%)
    all_to_all x1, blocking collectives, shards(): lax.all_to_all(send, 'z', split_axis=0, concat_axis=0, tiled=True, axis_i...  26.1 us
    all_to_all x1, blocking collectives, shards(): lax.all_to_all(best, ('z', 'x', 'core'), split_axis=0, concat_axis=0, til...  19.6 us
    all_to_all x1, blocking collectives, shards(): lax.all_to_all(send.reshape(COLUMNS * HELPERS, lines, LANES), ('x', 'core...  16.9 us

profile of v8, /device:TPU:1, one launch (start us, length us, event | category | flops | bytes accessed | tf_op | source)
XLA Modules:
  0.0 67.3 jit_solution(2048697031014186771)
XLA Ops:
  0.6 0.0 copy-start
  0.6 0.0 copy-start.3
  0.7 0.9 %add_bitcast_fusion.packed_ref = s32[18,128]{1,0:T(8,128)S(1)} fusion(s32[128]{0:T(128)} %param.9, s32[128]{0:T(128)} %param.7, s32[2048]{0:T(1024)} %param.8), kind=kLoop, calls=%fused_computation.2 | loop fusion | flops 4608 | bytes 18432 | tf_op jit(solution)/shard_map/reshape | solution.py:156
  1.5 0.5 index.1
  2.1 0.2 copy-done
  2.3 0.3 copy-done.3
  2.5 0.5 multiply_reduce_fusion
  3.1 0.0 copy-start.2
  3.1 0.1 multiply_convert_fusion.prefix_ref
  3.2 0.0 copy-start.1
  3.2 0.2 scatter.1
  3.4 26.1 %all_to_all.21.got_ref = bf16[16,9,4,128]{3,2,1,0:T(4,128)(2,1)S(1)} all-to-all(bf16[16,9,4,128]{3,2,1,0:T(4,128)(2,1)S(1)} %scatter.1), channel_id=1, replica_groups={{256,288,320,352,384,416,448,480,0,32,64,96,128,160,192,224},{257,289,3..., dimensions={0} | all-to-all | bytes 294912 | tf_op jit(solution)/shard_map/all_to_all | solution.py:183
  29.5 0.3 sort.1
  29.8 16.9 %all_to_all.22 = bf16[32,72,128]{2,1,0:T(8,128)(2,1)S(1)} all-to-all(bf16[32,72,128]{2,1,0:T(8,128)(2,1)S(1)} %bitcast.12), channel_id=1, replica_groups={{22,23,20,21,18,19,16,17,30,31,28,29,26,27,24,25,6,7,4,5,2,3,0,1,14,15,..., dimensions={0} | all-to-all | bytes 1179648 | tf_op jit(solution)/shard_map/all_to_all | solution.py:197
  46.7 0.4 best.1
  47.1 19.6 %all_to_all.23 = f32[128,1,128]{2,1,0:T(1,128)S(1)} all-to-all(f32[128,1,128]{2,1,0:T(1,128)S(1)} %bitcast.14), channel_id=1, replica_groups={{276,308,340,372,404,436,468,500,20,52,84,116,148,180,212,244,272,304,3..., dimensions={0} | all-to-all | bytes 131072 | tf_op jit(solution)/shard_map/all_to_all | solution.py:219
  66.7 0.0 copy-done.2
  66.7 0.6 finish.1
  67.3 0.0 copy-done.1
  (1 shorter events, 0.0 us)
Async XLA Ops:
  0.6 1.6 %copy-start = (bf16[4096,256]{1,0:T(8,128)(2,1)S(1)}, bf16[4096,256]{1,0:T(8,128)(2,1)}, u32[]{:S(2)}) copy-start(bf16[4096,256]{1,0:T(8,128)(2,1)} %param.6) | copy-start | bytes 6291460
  0.6 1.9 %copy-start.3 = (bf16[128,4096]{1,0:T(8,128)(2,1)S(1)}, bf16[128,4096]{1,0:T(8,128)(2,1)}, u32[]{:S(2)}) copy-start(bf16[128,4096]{1,0:T(8,128)(2,1)} %param.5) | copy-start | bytes 3145732
  3.1 63.6 %copy-start.2 = (s32[128]{0:T(128)S(1)}, s32[128]{0:T(128)}, u32[]{:S(2)}) copy-start(s32[128]{0:T(128)} %param.9) | copy-start | bytes 1540
  3.2 64.1 %copy-start.1 = (bf16[128,256]{1,0:T(8,128)(2,1)}, bf16[128,256]{1,0:T(8,128)(2,1)S(1)}, u32[]{:S(2)}) copy-start(bf16[128,256]{1,0:T(8,128)(2,1)S(1)} %multiply_convert_fusion.prefix_ref) | copy-start | bytes 196612

commit v9 on v8

--- a/solution.py
+++ b/solution.py
@@ -27,6 +27,15 @@
     return lax.broadcasted_iota(jnp.int32, shape, dim)
 
 
+def column_at(place):
+    return ((place & 3) * 2 + (place >> 2)) ^ COLUMN_TURN
+
+
+def place_of(column):
+    turned = column ^ COLUMN_TURN
+    return (turned & 1) * 4 + (turned >> 1)
+
+
 def hot(condition):
     return jnp.where(condition, 1.0, 0.0).astype(BF16)
 
@@ -53,7 +62,7 @@
     slot = jnp.sum(jnp.where(iota(square, 0) < iota(square, 1), same, 0.0), axis=0, keepdims=True)
     target = owner * SLOTS + slot.astype(jnp.int32)
     target = target ^ (PLANE_TURN * PLANE_SLOTS)
-    back = (((target >> 1) & 7) ^ COLUMN_TURN) * OWNER_SLOTS + (target >> 4) * SLOTS + (target & 1)
+    back = place_of((target >> 1) & 7) * OWNER_SLOTS + (target >> 4) * SLOTS + (target & 1)
     target_ref[...] = jnp.broadcast_to(back, target_ref.shape)
 
     live = packed_ref[17:18] == 1
@@ -71,32 +80,32 @@
     rows = jnp.concatenate([rows[:, :, :LANES], rows[:, :, LANES:]], axis=1)
     rows = rows.reshape(PLANES, PIECES, 8, LANES)
     labels = label_ref[...].reshape(PLANES, 1, 8, LANES)
-    send_ref[...] = jnp.concatenate(
-        [rows[:, :, :4], rows[:, :, 4:], labels[:, :, :4]], axis=1
-    ).astype(BF16)
+    parts = [rows[:, :, line : line + 2] for line in range(0, 8, 2)] + [labels[:, :, :2]]
+    send_ref[...] = jnp.concatenate(parts, axis=1).astype(BF16)
 
 
 def sort_kernel(got_ref, send_ref):
     helper = lax.axis_index("help") ^ HELPER_TURN
     pieces = got_ref[...].astype(F32)
-    got = jnp.concatenate([pieces[:, :PIECES], pieces[:, PIECES : 2 * PIECES]], axis=2)
+    got = [pieces[:, part * PIECES : (part + 1) * PIECES] for part in range(4)]
+    got = jnp.concatenate(got, axis=2)
     got = got.reshape(PLANES, 2 * PLANE_SLOTS, LANES)
     low = got[:, :PLANE_SLOTS].reshape(SLAB, LANES).astype(BF16)
     high = got[:, PLANE_SLOTS:].reshape(SLAB, LANES).astype(BF16)
     dest = iota((SLAB, SLAB), 0)
-    source = (dest & 15) * PLANE_SLOTS + ((dest >> 5) ^ COLUMN_TURN) * SLOTS + ((dest >> 4) & 1)
+    source = (dest & 15) * PLANE_SLOTS + column_at(dest >> 5) * SLOTS + ((dest >> 4) & 1)
     order = hot(iota((SLAB, SLAB), 1) == source)
     rows = dot(order, jnp.concatenate([low, high], axis=1))
     rows = rows.reshape(COLUMNS, OWNER_SLOTS, 2 * LANES)
 
-    tiles = pieces[:, 2 * PIECES].reshape(PLANES, 4, LANES)
-    tiles = jnp.concatenate([tiles, tiles], axis=1).reshape(PLANES * 8, LANES).astype(BF16)
+    tiles = jnp.concatenate([pieces[:, 4 * PIECES]] * 4, axis=1)
+    tiles = tiles.reshape(PLANES * 8, LANES).astype(BF16)
     line, lane = iota((2 * LANES, LANES), 0), iota((2 * LANES, LANES), 1)
     mine = ((line >> 5) & 3) == helper
     spread = dot(hot((lane == (line & 15) * 8 + (line >> 7)) & mine), tiles)
     spread = jnp.where((lane & 1) == ((line >> 4) & 1), spread, 0.0).astype(BF16)
     group = (COLUMNS * 8, LANES)
-    labels = dot_nt(hot((iota(group, 1) >> 1) == ((iota(group, 0) >> 3) ^ COLUMN_TURN)), spread)
+    labels = dot_nt(hot((iota(group, 1) >> 1) == column_at(iota(group, 0) >> 3)), spread)
     labels = jnp.where((iota(group, 0) & 7) < 4, labels[:, :LANES], labels[:, LANES:])
     labels = labels.reshape(COLUMNS, 8, LANES)
     out = jnp.concatenate([rows[:, :, :LANES], rows[:, :, LANES:], labels], axis=1).astype(BF16)
@@ -173,7 +182,7 @@
     prefix = (projected * norm).astype(BF16)
     send = pl.pallas_call(
         scatter_kernel,
-        out_shape=jax.ShapeDtypeStruct((PLANES, 2 * PIECES + 1, 4, LANES), BF16),
+        out_shape=jax.ShapeDtypeStruct((PLANES, 4 * PIECES + 1, 2, LANES), BF16),
         in_specs=[VMEM] * 3,
         out_specs=VMEM,
         compiler_params=LIMIT,
@@ -192,8 +201,12 @@
         compiler_params=LIMIT,
         name="sort",
     )(got)
-    turn = COLUMN_TURN * HELPERS + HELPER_TURN
-    members = [[spot ^ turn for spot in range(COLUMNS * HELPERS)]]
+    members = [
+        [
+            column_at(spot // HELPERS) * HELPERS + (spot % HELPERS ^ HELPER_TURN)
+            for spot in range(COLUMNS * HELPERS)
+        ]
+    ]
     got = lax.all_to_all(
         send.reshape(COLUMNS * HELPERS, lines, LANES),
         ("x", "core", "help"),
@@ -212,7 +225,7 @@
     )(got.reshape(COLUMNS, HELPERS, lines, LANES))
     owners = [
         [
-            (spot % PLANES ^ PLANE_TURN) * COLUMNS + (spot // PLANES ^ COLUMN_TURN)
+            (spot % PLANES ^ PLANE_TURN) * COLUMNS + column_at(spot // PLANES)
             for spot in range(PLANES * COLUMNS)
         ]
     ]

time: 67.5 us -> 66.8 us (0.990)
  blocking collectives: 62.5 us -> 61.6 us
where the time goes in v9:
time: 66.8 us; the launch traced here: 66.5 us
  blocking collectives  61.6 us (92%)
  Pallas kernels  2.15 us (3%)
  other arithmetic  0.98 us (1%)
  between operations  0.71 us (1%)
    all_to_all x1, blocking collectives, shards(): lax.all_to_all(send, 'z', split_axis=0, concat_axis=0, tiled=True, axis_i...  25.7 us
    all_to_all x1, blocking collectives, shards(): lax.all_to_all(best, ('z', 'x', 'core'), split_axis=0, concat_axis=0, til...  19 us
    all_to_all x1, blocking collectives, shards(): lax.all_to_all(send.reshape(COLUMNS * HELPERS, lines, LANES), ('x', 'core...  17 us

profile of v9, /device:TPU:1, one launch (start us, length us, event | category | flops | bytes accessed | tf_op | source)
XLA Modules:
  0.0 66.5 jit_solution(4767523840285301889)
XLA Ops:
  0.6 0.0 copy-start
  0.6 0.0 copy-start.3
  0.7 0.9 %add_bitcast_fusion.packed_ref = s32[18,128]{1,0:T(8,128)S(1)} fusion(s32[128]{0:T(128)} %param.9, s32[128]{0:T(128)} %param.7, s32[2048]{0:T(1024)} %param.8), kind=kLoop, calls=%fused_computation.2 | loop fusion | flops 4608 | bytes 18432 | tf_op jit(solution)/shard_map/reshape | solution.py:165
  1.5 0.5 index.1
  2.1 0.2 copy-done
  2.3 0.3 copy-done.3
  2.5 0.5 multiply_reduce_fusion
  3.1 0.0 copy-start.2
  3.1 0.1 multiply_convert_fusion.prefix_ref
  3.2 0.0 copy-start.1
  3.2 0.2 scatter.1
  3.4 25.7 %all_to_all.21.got_ref = bf16[16,17,2,128]{3,2,1,0:T(2,128)(2,1)S(1)} all-to-all(bf16[16,17,2,128]{3,2,1,0:T(2,128)(2,1)S(1)} %scatter.1), channel_id=1, replica_groups={{256,288,320,352,384,416,448,480,0,32,64,96,128,160,192,224},{257,289,3..., dimensions={0} | all-to-all | bytes 278528 | tf_op jit(solution)/shard_map/all_to_all | solution.py:192
  29.1 0.4 sort.1
  29.5 17.0 %all_to_all.22 = bf16[32,72,128]{2,1,0:T(8,128)(2,1)S(1)} all-to-all(bf16[32,72,128]{2,1,0:T(8,128)(2,1)S(1)} %bitcast.12), channel_id=1, replica_groups={{22,23,20,21,30,31,28,29,6,7,4,5,14,15,12,13,18,19,16,17,26,27,24,25,2,..., dimensions={0} | all-to-all | bytes 1179648 | tf_op jit(solution)/shard_map/all_to_all | solution.py:210
  46.5 0.4 best.1
  46.9 19.0 %all_to_all.23 = f32[128,1,128]{2,1,0:T(1,128)S(1)} all-to-all(f32[128,1,128]{2,1,0:T(1,128)S(1)} %bitcast.14), channel_id=1, replica_groups={{276,308,340,372,404,436,468,500,20,52,84,116,148,180,212,244,284,316,3..., dimensions={0} | all-to-all | bytes 131072 | tf_op jit(solution)/shard_map/all_to_all | solution.py:232
  65.9 0.0 copy-done.2
  65.9 0.6 finish.1
  66.5 0.0 copy-done.1
  (1 shorter events, 0.0 us)
Async XLA Ops:
  0.6 1.6 %copy-start = (bf16[4096,256]{1,0:T(8,128)(2,1)S(1)}, bf16[4096,256]{1,0:T(8,128)(2,1)}, u32[]{:S(2)}) copy-start(bf16[4096,256]{1,0:T(8,128)(2,1)} %param.6) | copy-start | bytes 6291460
  0.6 1.9 %copy-start.3 = (bf16[128,4096]{1,0:T(8,128)(2,1)S(1)}, bf16[128,4096]{1,0:T(8,128)(2,1)}, u32[]{:S(2)}) copy-start(bf16[128,4096]{1,0:T(8,128)(2,1)} %param.5) | copy-start | bytes 3145732
  3.1 62.8 %copy-start.2 = (s32[128]{0:T(128)S(1)}, s32[128]{0:T(128)}, u32[]{:S(2)}) copy-start(s32[128]{0:T(128)} %param.9) | copy-start | bytes 1540
  3.2 63.3 %copy-start.1 = (bf16[128,256]{1,0:T(8,128)(2,1)}, bf16[128,256]{1,0:T(8,128)(2,1)S(1)}, u32[]{:S(2)}) copy-start(bf16[128,256]{1,0:T(8,128)(2,1)S(1)} %multiply_convert_fusion.prefix_ref) | copy-start | bytes 196612

commit v10 on v9

--- a/solution.py
+++ b/solution.py
@@ -14,6 +14,7 @@
 PLANE_SLOTS = COLUMNS * SLOTS
 SLAB = PLANES * PLANE_SLOTS
 OWNER_SLOTS = PLANES * SLOTS
+CHUNK = 2 * OWNER_SLOTS + 2
 PIECES = 2 * PLANE_SLOTS // 8
 PLANE_TURN = 8
 COLUMN_TURN = 5
@@ -106,28 +107,45 @@
     spread = jnp.where((lane & 1) == ((line >> 4) & 1), spread, 0.0).astype(BF16)
     group = (COLUMNS * 8, LANES)
     labels = dot_nt(hot((iota(group, 1) >> 1) == column_at(iota(group, 0) >> 3)), spread)
-    labels = jnp.where((iota(group, 0) & 7) < 4, labels[:, :LANES], labels[:, LANES:])
+    labels = jnp.where((iota(group, 0) & 7) == 0, labels[:, :LANES], labels[:, LANES:])
     labels = labels.reshape(COLUMNS, 8, LANES)
-    out = jnp.concatenate([rows[:, :, :LANES], rows[:, :, LANES:], labels], axis=1).astype(BF16)
-    for helper in range(HELPERS):
-        send_ref[:, helper] = out
+    parts = []
+    for column in range(COLUMNS):
+        chunk = [rows[column, :, :LANES], rows[column, :, LANES:], labels[column, :2]]
+        parts += [part.astype(BF16) for part in chunk] * HELPERS
+    send_ref[...] = jnp.concatenate(parts, axis=0)
 
 
 def best_kernel(got_ref, out_ref):
     helper = lax.axis_index("help") ^ HELPER_TURN
-    total = COLUMNS * HELPERS * OWNER_SLOTS
-    low = got_ref[:, :, :OWNER_SLOTS].reshape(total, LANES)
-    high = got_ref[:, :, OWNER_SLOTS : 2 * OWNER_SLOTS].reshape(total, LANES)
-
-    own = got_ref[:, helper, : 2 * OWNER_SLOTS].reshape(COLUMNS, 2 * SLOTS, PLANES, LANES)
-    parts = [own[:, part].reshape(COLUMNS * PLANES, LANES) for part in range(2 * SLOTS)]
+    got = got_ref[...]
+    lows, highs, owns, labels = [], [], [], []
+    for column in range(COLUMNS):
+        own = label = None
+        for place in range(HELPERS):
+            start = (column * HELPERS + place) * CHUNK
+            chunk = got[start : start + 2 * OWNER_SLOTS]
+            lows.append(chunk[:OWNER_SLOTS])
+            highs.append(chunk[OWNER_SLOTS:])
+            own = chunk if own is None else jnp.where(helper == place, chunk, own)
+            part = got[start + 2 * OWNER_SLOTS : start + CHUNK].astype(F32)
+            label = part if label is None else label + part
+        owns.append(own)
+        labels.append(label[0:1] * 128.0 + label[1:2])
+    columns = jnp.concatenate(
+        [jnp.concatenate(lows, axis=0), jnp.concatenate(highs, axis=0)], axis=1
+    )
+
+    parts = [
+        jnp.concatenate([own[part * PLANES : (part + 1) * PLANES] for own in owns], axis=0)
+        for part in range(2 * SLOTS)
+    ]
     own = jnp.concatenate(
         [jnp.concatenate(parts[:SLOTS], axis=0), jnp.concatenate(parts[SLOTS:], axis=0)], axis=1
     )
-    scores = dot_nt(own, jnp.concatenate([low, high], axis=1))
-
-    label = jnp.sum(got_ref[...].astype(F32)[:, :, 2 * OWNER_SLOTS :], axis=1)
-    label = label[:, 0:1] * 128.0 + label[:, 4:5]
+    scores = dot_nt(own, columns)
+
+    label = jnp.concatenate(labels, axis=0).reshape(COLUMNS, 1, LANES)
     shape = (SLOTS, COLUMNS, PLANES, LANES)
     small = (SLOTS, 1, PLANES, LANES)
     self_lane = iota(small, 3) == helper * OWNER_SLOTS + iota(small, 0) * PLANES + iota(small, 2)
@@ -192,10 +210,10 @@
     got = lax.all_to_all(
         send, "z", split_axis=0, concat_axis=0, tiled=True, axis_index_groups=planes
     )
-    lines = 2 * OWNER_SLOTS + 8
+    lines = COLUMNS * HELPERS * CHUNK
     send = pl.pallas_call(
         sort_kernel,
-        out_shape=jax.ShapeDtypeStruct((COLUMNS, HELPERS, lines, LANES), BF16),
+        out_shape=jax.ShapeDtypeStruct((lines, LANES), BF16),
         in_specs=[VMEM],
         out_specs=VMEM,
         compiler_params=LIMIT,
@@ -208,7 +226,7 @@
         ]
     ]
     got = lax.all_to_all(
-        send.reshape(COLUMNS * HELPERS, lines, LANES),
+        send.reshape(COLUMNS * HELPERS, CHUNK // 2, 2, LANES),
         ("x", "core", "help"),
         split_axis=0,
         concat_axis=0,
@@ -222,7 +240,7 @@
         out_specs=VMEM,
         compiler_params=LIMIT,
         name="best",
-    )(got.reshape(COLUMNS, HELPERS, lines, LANES))
+    )(got.reshape(lines, LANES))
     owners = [
         [
             (spot % PLANES ^ PLANE_TURN) * COLUMNS + column_at(spot // PLANES)

time: 66.8 us -> 66.4 us (level)
  no operation moved by 1% of the time
where the time goes in v10:
time: 66.4 us; the launch traced here: 66.2 us
  blocking collectives  61.1 us (92%)
  Pallas kernels  2.31 us (3%)
  other arithmetic  0.98 us (1%)
  between operations  0.71 us (1%)
    all_to_all x1, blocking collectives, shards(): lax.all_to_all(send, 'z', split_axis=0, concat_axis=0, tiled=True, axis_i...  25.7 us
    all_to_all x1, blocking collectives, shards(): lax.all_to_all(best, ('z', 'x', 'core'), split_axis=0, concat_axis=0, til...  19 us
    all_to_all x1, blocking collectives, shards(): lax.all_to_all(send.reshape(COLUMNS * HELPERS, CHUNK // 2, 2, LANES), ('x...  16.4 us

profile of v10, /device:TPU:1, one launch (start us, length us, event | category | flops | bytes accessed | tf_op | source)
XLA Modules:
  0.0 66.2 jit_solution(14255406944814202209)
XLA Ops:
  0.6 0.0 copy-start
  0.6 0.0 copy-start.3
  0.7 0.9 %add_bitcast_fusion.packed_ref = s32[18,128]{1,0:T(8,128)S(1)} fusion(s32[128]{0:T(128)} %param.9, s32[128]{0:T(128)} %param.7, s32[2048]{0:T(1024)} %param.8), kind=kLoop, calls=%fused_computation.2 | loop fusion | flops 4608 | bytes 18432 | tf_op jit(solution)/shard_map/reshape | solution.py:183
  1.5 0.5 index.1
  2.1 0.2 copy-done
  2.3 0.3 copy-done.3
  2.5 0.5 multiply_reduce_fusion
  3.1 0.0 copy-start.2
  3.1 0.1 multiply_convert_fusion.prefix_ref
  3.2 0.0 copy-start.1
  3.2 0.2 scatter.1
  3.4 25.7 %all_to_all.21.got_ref = bf16[16,17,2,128]{3,2,1,0:T(2,128)(2,1)S(1)} all-to-all(bf16[16,17,2,128]{3,2,1,0:T(2,128)(2,1)S(1)} %scatter.1), channel_id=1, replica_groups={{256,288,320,352,384,416,448,480,0,32,64,96,128,160,192,224},{257,289,3..., dimensions={0} | all-to-all | bytes 278528 | tf_op jit(solution)/shard_map/all_to_all | solution.py:210
  29.1 0.4 sort.1
  29.5 16.4 %all_to_all.22 = bf16[32,33,2,128]{3,2,1,0:T(2,128)(2,1)S(1)} all-to-all(bf16[32,33,2,128]{3,2,1,0:T(2,128)(2,1)S(1)} %bitcast.12), channel_id=1, replica_groups={{22,23,20,21,30,31,28,29,6,7,4,5,14,15,12,13,18,19,16,17,26,27,24,25,2,..., dimensions={0} | all-to-all | bytes 1081344 | tf_op jit(solution)/shard_map/all_to_all | solution.py:228
  45.9 0.5 best.1
  46.5 19.0 %all_to_all.23 = f32[128,1,128]{2,1,0:T(1,128)S(1)} all-to-all(f32[128,1,128]{2,1,0:T(1,128)S(1)} %bitcast.14), channel_id=1, replica_groups={{276,308,340,372,404,436,468,500,20,52,84,116,148,180,212,244,284,316,3..., dimensions={0} | all-to-all | bytes 131072 | tf_op jit(solution)/shard_map/all_to_all | solution.py:250
  65.5 0.0 copy-done.2
  65.5 0.6 finish.1
  66.2 0.0 copy-done.1
  (1 shorter events, 0.0 us)
Async XLA Ops:
  0.6 1.6 %copy-start = (bf16[4096,256]{1,0:T(8,128)(2,1)S(1)}, bf16[4096,256]{1,0:T(8,128)(2,1)}, u32[]{:S(2)}) copy-start(bf16[4096,256]{1,0:T(8,128)(2,1)} %param.6) | copy-start | bytes 6291460
  0.6 1.9 %copy-start.3 = (bf16[128,4096]{1,0:T(8,128)(2,1)S(1)}, bf16[128,4096]{1,0:T(8,128)(2,1)}, u32[]{:S(2)}) copy-start(bf16[128,4096]{1,0:T(8,128)(2,1)} %param.5) | copy-start | bytes 3145732
  3.1 62.5 %copy-start.2 = (s32[128]{0:T(128)S(1)}, s32[128]{0:T(128)}, u32[]{:S(2)}) copy-start(s32[128]{0:T(128)} %param.9) | copy-start | bytes 1540
  3.2 63.0 %copy-start.1 = (bf16[128,256]{1,0:T(8,128)(2,1)}, bf16[128,256]{1,0:T(8,128)(2,1)S(1)}, u32[]{:S(2)}) copy-start(bf16[128,256]{1,0:T(8,128)(2,1)S(1)} %multiply_convert_fusion.prefix_ref) | copy-start | bytes 196612

commit v11 on v10

--- a/solution.py
+++ b/solution.py
@@ -15,7 +15,7 @@
 SLAB = PLANES * PLANE_SLOTS
 OWNER_SLOTS = PLANES * SLOTS
 CHUNK = 2 * OWNER_SLOTS + 2
-PIECES = 2 * PLANE_SLOTS // 8
+PLANE_CHUNK = 2 * PLANE_SLOTS + 2
 PLANE_TURN = 8
 COLUMN_TURN = 5
 HELPER_TURN = 2
@@ -77,33 +77,31 @@
 
 
 def scatter_kernel(prefix_ref, hit_ref, label_ref, send_ref):
-    rows = dot(hit_ref[...], prefix_ref[...]).reshape(PLANES, PLANE_SLOTS, 2 * LANES)
-    rows = jnp.concatenate([rows[:, :, :LANES], rows[:, :, LANES:]], axis=1)
-    rows = rows.reshape(PLANES, PIECES, 8, LANES)
-    labels = label_ref[...].reshape(PLANES, 1, 8, LANES)
-    parts = [rows[:, :, line : line + 2] for line in range(0, 8, 2)] + [labels[:, :, :2]]
-    send_ref[...] = jnp.concatenate(parts, axis=1).astype(BF16)
+    rows = dot(hit_ref[...], prefix_ref[...]).astype(BF16)
+    labels = label_ref[...].astype(BF16)
+    parts = []
+    for plane in range(PLANES):
+        part = rows[plane * PLANE_SLOTS : (plane + 1) * PLANE_SLOTS]
+        parts += [part[:, :LANES], part[:, LANES:], labels[plane * 8 : plane * 8 + 2]]
+    send_ref[...] = jnp.concatenate(parts, axis=0)
 
 
 def sort_kernel(got_ref, send_ref):
     helper = lax.axis_index("help") ^ HELPER_TURN
-    pieces = got_ref[...].astype(F32)
-    got = [pieces[:, part * PIECES : (part + 1) * PIECES] for part in range(4)]
-    got = jnp.concatenate(got, axis=2)
-    got = got.reshape(PLANES, 2 * PLANE_SLOTS, LANES)
-    low = got[:, :PLANE_SLOTS].reshape(SLAB, LANES).astype(BF16)
-    high = got[:, PLANE_SLOTS:].reshape(SLAB, LANES).astype(BF16)
+    got = got_ref[...]
+    chunks = [got[plane * PLANE_CHUNK : (plane + 1) * PLANE_CHUNK] for plane in range(PLANES)]
+    low = jnp.concatenate([chunk[:PLANE_SLOTS] for chunk in chunks], axis=0)
+    high = jnp.concatenate([chunk[PLANE_SLOTS : 2 * PLANE_SLOTS] for chunk in chunks], axis=0)
     dest = iota((SLAB, SLAB), 0)
     source = (dest & 15) * PLANE_SLOTS + column_at(dest >> 5) * SLOTS + ((dest >> 4) & 1)
     order = hot(iota((SLAB, SLAB), 1) == source)
     rows = dot(order, jnp.concatenate([low, high], axis=1))
     rows = rows.reshape(COLUMNS, OWNER_SLOTS, 2 * LANES)
 
-    tiles = jnp.concatenate([pieces[:, 4 * PIECES]] * 4, axis=1)
-    tiles = tiles.reshape(PLANES * 8, LANES).astype(BF16)
+    tiles = jnp.concatenate([chunk[2 * PLANE_SLOTS :] for chunk in chunks], axis=0)
     line, lane = iota((2 * LANES, LANES), 0), iota((2 * LANES, LANES), 1)
     mine = ((line >> 5) & 3) == helper
-    spread = dot(hot((lane == (line & 15) * 8 + (line >> 7)) & mine), tiles)
+    spread = dot(hot((lane == (line & 15) * 2 + (line >> 7)) & mine)[:, : 2 * PLANES], tiles)
     spread = jnp.where((lane & 1) == ((line >> 4) & 1), spread, 0.0).astype(BF16)
     group = (COLUMNS * 8, LANES)
     labels = dot_nt(hot((iota(group, 1) >> 1) == column_at(iota(group, 0) >> 3)), spread)
@@ -200,13 +198,14 @@
     prefix = (projected * norm).astype(BF16)
     send = pl.pallas_call(
         scatter_kernel,
-        out_shape=jax.ShapeDtypeStruct((PLANES, 4 * PIECES + 1, 2, LANES), BF16),
+        out_shape=jax.ShapeDtypeStruct((PLANES * PLANE_CHUNK, LANES), BF16),
         in_specs=[VMEM] * 3,
         out_specs=VMEM,
         compiler_params=LIMIT,
         name="scatter",
     )(prefix, hit, label)
     planes = [[spot ^ PLANE_TURN for spot in range(PLANES)]]
+    send = send.reshape(PLANES, PLANE_CHUNK // 2, 2, LANES)
     got = lax.all_to_all(
         send, "z", split_axis=0, concat_axis=0, tiled=True, axis_index_groups=planes
     )
@@ -218,7 +217,7 @@
         out_specs=VMEM,
         compiler_params=LIMIT,
         name="sort",
-    )(got)
+    )(got.reshape(PLANES * PLANE_CHUNK, LANES))
     members = [
         [
             column_at(spot // HELPERS) * HELPERS + (spot % HELPERS ^ HELPER_TURN)

time: 66.4 us -> 66.3 us (level)
  no operation moved by 1% of the time
where the time goes in v11:
time: 66.3 us; the launch traced here: 66.1 us
  blocking collectives  61.1 us (92%)
  Pallas kernels  2.21 us (3%)
  other arithmetic  0.98 us (1%)
  between operations  0.71 us (1%)
    all_to_all x1, blocking collectives, shards(): lax.all_to_all(send, 'z', split_axis=0, concat_axis=0, tiled=True, axis_i...  25.7 us
    all_to_all x1, blocking collectives, shards(): lax.all_to_all(best, ('z', 'x', 'core'), split_axis=0, concat_axis=0, til...  19 us
    all_to_all x1, blocking collectives, shards(): lax.all_to_all(send.reshape(COLUMNS * HELPERS, CHUNK // 2, 2, LANES), ('x...  16.4 us

profile of v11, /device:TPU:1, one launch (start us, length us, event | category | flops | bytes accessed | tf_op | source)
XLA Modules:
  0.0 66.1 jit_solution(6547880864574948433)
XLA Ops:
  0.6 0.0 copy-start
  0.6 0.0 copy-start.3
  0.7 0.9 %add_bitcast_fusion.packed_ref = s32[18,128]{1,0:T(8,128)S(1)} fusion(s32[128]{0:T(128)} %param.9, s32[128]{0:T(128)} %param.7, s32[2048]{0:T(1024)} %param.8), kind=kLoop, calls=%fused_computation.2 | loop fusion | flops 4608 | bytes 18432 | tf_op jit(solution)/shard_map/reshape | solution.py:181
  1.5 0.5 index.1
  2.1 0.2 copy-done
  2.3 0.3 copy-done.3
  2.5 0.5 multiply_reduce_fusion
  3.1 0.0 copy-start.2
  3.1 0.1 multiply_convert_fusion.prefix_ref
  3.2 0.0 copy-start.1
  3.2 0.2 scatter.1
  3.4 25.7 %all_to_all.21 = bf16[16,17,2,128]{3,2,1,0:T(2,128)(2,1)S(1)} all-to-all(bf16[16,17,2,128]{3,2,1,0:T(2,128)(2,1)S(1)} %bitcast.16), channel_id=1, replica_groups={{256,288,320,352,384,416,448,480,0,32,64,96,128,160,192,224},{257,289,3..., dimensions={0} | all-to-all | bytes 278528 | tf_op jit(solution)/shard_map/all_to_all | solution.py:209
  29.1 0.4 sort.1
  29.4 16.4 %all_to_all.22 = bf16[32,33,2,128]{3,2,1,0:T(2,128)(2,1)S(1)} all-to-all(bf16[32,33,2,128]{3,2,1,0:T(2,128)(2,1)S(1)} %bitcast.14), channel_id=1, replica_groups={{22,23,20,21,30,31,28,29,6,7,4,5,14,15,12,13,18,19,16,17,26,27,24,25,2,..., dimensions={0} | all-to-all | bytes 1081344 | tf_op jit(solution)/shard_map/all_to_all | solution.py:227
  45.9 0.5 best.1
  46.4 19.0 %all_to_all.23 = f32[128,1,128]{2,1,0:T(1,128)S(1)} all-to-all(f32[128,1,128]{2,1,0:T(1,128)S(1)} %bitcast.18), channel_id=1, replica_groups={{276,308,340,372,404,436,468,500,20,52,84,116,148,180,212,244,284,316,3..., dimensions={0} | all-to-all | bytes 131072 | tf_op jit(solution)/shard_map/all_to_all | solution.py:249
  65.4 0.0 copy-done.2
  65.4 0.6 finish.1
  66.1 0.0 copy-done.1
  (1 shorter events, 0.0 us)
Async XLA Ops:
  0.6 1.6 %copy-start = (bf16[4096,256]{1,0:T(8,128)(2,1)S(1)}, bf16[4096,256]{1,0:T(8,128)(2,1)}, u32[]{:S(2)}) copy-start(bf16[4096,256]{1,0:T(8,128)(2,1)} %param.6) | copy-start | bytes 6291460
  0.6 1.9 %copy-start.3 = (bf16[128,4096]{1,0:T(8,128)(2,1)S(1)}, bf16[128,4096]{1,0:T(8,128)(2,1)}, u32[]{:S(2)}) copy-start(bf16[128,4096]{1,0:T(8,128)(2,1)} %param.5) | copy-start | bytes 3145732
  3.1 62.4 %copy-start.2 = (s32[128]{0:T(128)S(1)}, s32[128]{0:T(128)}, u32[]{:S(2)}) copy-start(s32[128]{0:T(128)} %param.9) | copy-start | bytes 1540
  3.2 62.9 %copy-start.1 = (bf16[128,256]{1,0:T(8,128)(2,1)}, bf16[128,256]{1,0:T(8,128)(2,1)S(1)}, u32[]{:S(2)}) copy-start(bf16[128,256]{1,0:T(8,128)(2,1)S(1)} %multiply_convert_fusion.prefix_ref) | copy-start | bytes 196612

commit v12 on v11

--- a/solution.py
+++ b/solution.py
@@ -62,7 +62,7 @@
     )
     slot = jnp.sum(jnp.where(iota(square, 0) < iota(square, 1), same, 0.0), axis=0, keepdims=True)
     target = owner * SLOTS + slot.astype(jnp.int32)
-    target = target ^ (PLANE_TURN * PLANE_SLOTS)
+    target = ((PLANE_TURN - (target >> 4)) & (PLANES - 1)) * PLANE_SLOTS + (target & (PLANE_SLOTS - 1))
     back = place_of((target >> 1) & 7) * OWNER_SLOTS + (target >> 4) * SLOTS + (target & 1)
     target_ref[...] = jnp.broadcast_to(back, target_ref.shape)
 
@@ -204,7 +204,7 @@
         compiler_params=LIMIT,
         name="scatter",
     )(prefix, hit, label)
-    planes = [[spot ^ PLANE_TURN for spot in range(PLANES)]]
+    planes = [[(PLANE_TURN - spot) % PLANES for spot in range(PLANES)]]
     send = send.reshape(PLANES, PLANE_CHUNK // 2, 2, LANES)
     got = lax.all_to_all(
         send, "z", split_axis=0, concat_axis=0, tiled=True, axis_index_groups=planes
@@ -242,7 +242,7 @@
     )(got.reshape(lines, LANES))
     owners = [
         [
-            (spot % PLANES ^ PLANE_TURN) * COLUMNS + column_at(spot // PLANES)
+            ((PLANE_TURN - spot) % PLANES) * COLUMNS + column_at(spot // PLANES)
             for spot in range(PLANES * COLUMNS)
         ]
     ]

time: 66.3 us -> 66.3 us (level)
  no operation moved by 1% of the time
where the time goes in v12:
time: 66.3 us; the launch traced here: 66.1 us
  blocking collectives  61.2 us (92%)
  Pallas kernels  2.22 us (3%)
  other arithmetic  0.98 us (1%)
  between operations  0.71 us (1%)
    all_to_all x1, blocking collectives, shards(): lax.all_to_all(send, 'z', split_axis=0, concat_axis=0, tiled=True, axis_i...  26 us
    all_to_all x1, blocking collectives, shards(): lax.all_to_all(best, ('z', 'x', 'core'), split_axis=0, concat_axis=0, til...  19.1 us
    all_to_all x1, blocking collectives, shards(): lax.all_to_all(send.reshape(COLUMNS * HELPERS, CHUNK // 2, 2, LANES), ('x...  16.1 us

profile of v12, /device:TPU:1, one launch (start us, length us, event | category | flops | bytes accessed | tf_op | source)
XLA Modules:
  0.0 66.1 jit_solution(15900750080544064501)
XLA Ops:
  0.6 0.0 copy-start
  0.6 0.0 copy-start.3
  0.7 0.9 %add_bitcast_fusion.packed_ref = s32[18,128]{1,0:T(8,128)S(1)} fusion(s32[128]{0:T(128)} %param.9, s32[128]{0:T(128)} %param.7, s32[2048]{0:T(1024)} %param.8), kind=kLoop, calls=%fused_computation.2 | loop fusion | flops 4608 | bytes 18432 | tf_op jit(solution)/shard_map/reshape | solution.py:181
  1.5 0.5 index.1
  2.1 0.2 copy-done
  2.3 0.3 copy-done.3
  2.5 0.5 multiply_reduce_fusion
  3.1 0.0 copy-start.2
  3.1 0.1 multiply_convert_fusion.prefix_ref
  3.2 0.0 copy-start.1
  3.2 0.2 scatter.1
  3.4 26.0 %all_to_all.21 = bf16[16,17,2,128]{3,2,1,0:T(2,128)(2,1)S(1)} all-to-all(bf16[16,17,2,128]{3,2,1,0:T(2,128)(2,1)S(1)} %bitcast.16), channel_id=1, replica_groups={{256,224,192,160,128,96,64,32,0,480,448,416,384,352,320,288},{257,225,1..., dimensions={0} | all-to-all | bytes 278528 | tf_op jit(solution)/shard_map/all_to_all | solution.py:209
  29.4 0.4 sort.1
  29.7 16.1 %all_to_all.22 = bf16[32,33,2,128]{3,2,1,0:T(2,128)(2,1)S(1)} all-to-all(bf16[32,33,2,128]{3,2,1,0:T(2,128)(2,1)S(1)} %bitcast.14), channel_id=1, replica_groups={{22,23,20,21,30,31,28,29,6,7,4,5,14,15,12,13,18,19,16,17,26,27,24,25,2,..., dimensions={0} | all-to-all | bytes 1081344 | tf_op jit(solution)/shard_map/all_to_all | solution.py:227
  45.8 0.5 best.1
  46.4 19.1 %all_to_all.23 = f32[128,1,128]{2,1,0:T(1,128)S(1)} all-to-all(f32[128,1,128]{2,1,0:T(1,128)S(1)} %bitcast.18), channel_id=1, replica_groups={{276,244,212,180,148,116,84,52,20,500,468,436,404,372,340,308,284,252,2..., dimensions={0} | all-to-all | bytes 131072 | tf_op jit(solution)/shard_map/all_to_all | solution.py:249
  65.5 0.0 copy-done.2
  65.5 0.6 finish.1
  66.1 0.0 copy-done.1
  (1 shorter events, 0.0 us)
Async XLA Ops:
  0.6 1.6 %copy-start = (bf16[4096,256]{1,0:T(8,128)(2,1)S(1)}, bf16[4096,256]{1,0:T(8,128)(2,1)}, u32[]{:S(2)}) copy-start(bf16[4096,256]{1,0:T(8,128)(2,1)} %param.6) | copy-start | bytes 6291460
  0.6 1.9 %copy-start.3 = (bf16[128,4096]{1,0:T(8,128)(2,1)S(1)}, bf16[128,4096]{1,0:T(8,128)(2,1)}, u32[]{:S(2)}) copy-start(bf16[128,4096]{1,0:T(8,128)(2,1)} %param.5) | copy-start | bytes 3145732
  3.1 62.4 %copy-start.2 = (s32[128]{0:T(128)S(1)}, s32[128]{0:T(128)}, u32[]{:S(2)}) copy-start(s32[128]{0:T(128)} %param.9) | copy-start | bytes 1540
  3.2 62.9 %copy-start.1 = (bf16[128,256]{1,0:T(8,128)(2,1)}, bf16[128,256]{1,0:T(8,128)(2,1)S(1)}, u32[]{:S(2)}) copy-start(bf16[128,256]{1,0:T(8,128)(2,1)S(1)} %multiply_convert_fusion.prefix_ref) | copy-start | bytes 196612
